TPU v7x, 32 devices: a whole 2x2x4 slice. The times are simulated.
32 devices in a mesh: row: 8 (over y, x, core), col: 4 (over z).
Axes of the slice: x: 2, y: 2, z: 4, core: 2. Of those that a mesh axis runs over, the one named last changes fastest.
Arguments:
- ratings: bfloat16 [4, 65536, 512], P(None, ('row', 'col'))
- tile_mask: int32 [4, 512, 4], P(None, ('row', 'col')), may hold values from 0 to 1, as said below
- tile_counts: int32 [32], replicated, may hold values from 1 to 16, as said below
- users: float32 [32768, 128], P(('row', 'col')), may hold values from -2 to 2
- user_accum: float32 [32768, 128], P(('row', 'col')), may hold values from 0.05 to 0.5
- items: float32 [16384, 128], P(('row', 'col')), may hold values from -2 to 2
- item_accum: float32 [16384, 128], P(('row', 'col')), may hold values from 0.05 to 0.5
Outputs:
- users_out: float32 [32768, 128], P(('row', 'col'))
- user_accum_out: float32 [32768, 128], P(('row', 'col'))
- items_out: float32 [16384, 128], P(('row', 'col'))
- item_accum_out: float32 [16384, 128], P(('row', 'col'))
- losses: float32 [4], replicated
Inputs may be any that keep to these rules, and one draw needn't show every extreme that they name: Each group of 4 positions has tile_counts summing to 32, and exactly one position of each group, not always the same, owns 2 * 8 tiles. `tile_mask`: in each stratum, the first slot's first item tile of every position is 1.
All inputs are finite; a program needn't handle non-finite values.
Results may differ from a plain program's by a relative error of at most 0.0025.
Values sent between devices are 32-bit elements; how exact they have to be, the bound alone decides.
A program may use at most 64 MiB of HBM per device.

v0:
```python
import jax
import jax.numpy as jnp
from jax import lax
from jax.sharding import PartitionSpec as P

TILE = 128
UT = 8
STEPS = 3


ridge_weight = 0.02
step_rate = 0.05


def passed_along(value, axis, steps):
    count = lax.axis_size(axis)
    pairs = [(source, (source + steps) % count) for source in range(count)]
    return lax.ppermute(value, axis, pairs)


def update(user_fac, user_acc, item_fac, item_acc, rating_block, live_tiles):
    tile_size = user_fac.shape[0] // live_tiles.shape[0]
    user_half = user_fac.astype(jnp.bfloat16)
    item_half = item_fac.astype(jnp.bfloat16)
    predicted = lax.dot_general(
        user_half, item_half, (((1,), (1,)), ((), ())), preferred_element_type=jnp.float32
    )
    residue = predicted - rating_block.astype(jnp.float32)
    masked = (
        residue.reshape(live_tiles.shape[0], tile_size, live_tiles.shape[1], tile_size)
        * live_tiles[:, None, :, None]
    ).reshape(residue.shape)
    sq_error = jnp.sum(masked * residue)
    err_half = masked.astype(jnp.bfloat16)
    grad_user = (
        jnp.dot(err_half, item_half, preferred_element_type=jnp.float32)
        * float(item_fac.shape[0]) ** (-0.5)
        + ridge_weight * user_fac
    )
    grad_item = (
        lax.dot_general(
            err_half, user_half, (((0,), (0,)), ((), ())), preferred_element_type=jnp.float32
        )
        * float(UT * TILE) ** (-0.5)
        + ridge_weight * item_fac
    )
    user_acc = user_acc + grad_user * grad_user
    item_acc = item_acc + grad_item * grad_item
    user_fac = user_fac - step_rate * grad_user * lax.rsqrt(user_acc)
    item_fac = item_fac - step_rate * grad_item * lax.rsqrt(item_acc)
    return (user_fac, user_acc, item_fac, item_acc, sq_error)


def on_device(ratings, tile_mask, tile_counts, users, user_accum, items, item_accum):
    strata_count = ratings.shape[0]
    slot_count = tile_mask.shape[1]
    tile_size = ratings.shape[1] // slot_count
    group_size = lax.axis_size("col")
    member = lax.axis_index("col")
    arrived_rows = users.shape[0]
    group_counts = lax.dynamic_slice_in_dim(
        tile_counts, lax.axis_index("row") * group_size, group_size
    )
    ranks = jnp.arange(group_size, dtype=jnp.int32)
    start_tile = jnp.sum(jnp.where(ranks < member, group_counts, 0))
    own_count = jnp.sum(jnp.where(ranks == member, group_counts, 0))
    valid = (jnp.arange(slot_count, dtype=jnp.int32) < own_count).astype(jnp.float32)
    whole_fac, whole_acc = (
        lax.all_gather(users, "col", axis=0, tiled=True),
        lax.all_gather(user_accum, "col", axis=0, tiled=True),
    )
    pad_rows = slot_count * tile_size
    ext_fac = jnp.concatenate([whole_fac, whole_fac[:pad_rows]], axis=0)
    ext_acc = jnp.concatenate([whole_acc, whole_acc[:pad_rows]], axis=0)
    user_fac = lax.dynamic_slice_in_dim(ext_fac, start_tile * tile_size, pad_rows, 0)
    user_acc = lax.dynamic_slice_in_dim(ext_acc, start_tile * tile_size, pad_rows, 0)
    held_pair = jnp.stack([items, item_accum])
    loss_list = []
    for stratum in range(strata_count):
        live_tiles = tile_mask[stratum].astype(jnp.float32) * valid[:, None]
        item_fac = held_pair[0]
        item_acc = held_pair[1]
        for inner in range(STEPS):
            user_fac, user_acc, item_fac, item_acc, sq_error = update(
                user_fac, user_acc, item_fac, item_acc, ratings[stratum], live_tiles
            )
            if inner == 0:
                observed = jnp.sum(live_tiles) * float(tile_size * tile_size)
                total_error, total_count = lax.psum((sq_error, observed), ("row", "col"))
                loss_list.append(total_error / total_count)
        held_pair = jnp.stack([item_fac, item_acc])
        if stratum + 1 < strata_count:
            held_pair = passed_along(held_pair, ("row", "col"), 1)
    losses = jnp.stack(loss_list)
    row_valid = jnp.repeat(valid, tile_size)[:, None] > 0.5
    kept_fac = jnp.where(row_valid, user_fac, 0.0)
    kept_acc = jnp.where(row_valid, user_acc, 0.0)
    frame_rows = group_size * arrived_rows + pad_rows
    frame_fac = lax.dynamic_update_slice_in_dim(
        jnp.zeros((frame_rows, kept_fac.shape[1]), jnp.float32), kept_fac, start_tile * tile_size, 0
    )
    frame_acc = lax.dynamic_update_slice_in_dim(
        jnp.zeros((frame_rows, kept_acc.shape[1]), jnp.float32), kept_acc, start_tile * tile_size, 0
    )
    users_new, accum_new = (
        lax.psum_scatter(
            frame_fac[: group_size * arrived_rows], "col", scatter_dimension=0, tiled=True
        ),
        lax.psum_scatter(
            frame_acc[: group_size * arrived_rows], "col", scatter_dimension=0, tiled=True
        ),
    )
    return (users_new, accum_new, held_pair[0], held_pair[1], losses)


def solution(mesh):
    return jax.shard_map(
        on_device,
        mesh=mesh,
        in_specs=(
            P(None, ("row", "col"), None),
            P(None, ("row", "col"), None),
            P(),
            P(("row", "col"), None),
            P(("row", "col"), None),
            P(("row", "col"), None),
            P(("row", "col"), None),
        ),
        out_specs=(
            P(("row", "col"), None),
            P(("row", "col"), None),
            P(("row", "col"), None),
            P(("row", "col"), None),
            P(),
        ),
        check_vma=False,
    )
```

profile of v0, /device:TPU:0, one launch (start us, length us, event | category | flops | bytes accessed | tf_op | source)
XLA Modules:
  0.0 308.9 jit_solution(11512856287630116489)
XLA Ops:
  12.9 45.4 %all-gather.3.cloned.1.call-done = f32[4096,128]{1,0:T(8,128)} async-done(((f32[1024,128]{1,0:T(8,128)}), f32[4096,128]{1,0:T(8,128)}) %all-gather.3.cloned.1.call-update) | async-done | bytes 2097168 | tf_op jit(solution)/shard_map/all_gather | solution.py:69
  62.1 4.7 %multiply_reduce_fusion.3 = (f32[]{:T(128)}, bf16[2048,512]{1,0:T(8,128)(2,1)S(1)}) fusion(f32[256,8,4,128]{3,2,1,0:T(4,128)S(1)} %bitcast.197, bf16[4,2048,512]{2,1,0:T(8,128)(2,1)} %param.7, f32[512,128]{1,0:T(8,128)S(1)} %copy-done.8, f32[2048,128]{1,0:T(8,128)S(1)} %fusion.37), kind=kOutput, calls=%fused_computation.35 | convolution fusion | flops 275054592 | bytes 9699332 | tf_op jit(solution)/shard_map/dot_general | solution.py:25
  68.2 36.3 %all-gather.5.cloned.1.call-done = f32[4096,128]{1,0:T(8,128)} async-done(((f32[1024,128]{1,0:T(8,128)}), f32[4096,128]{1,0:T(8,128)}) %all-gather.5.cloned.1.call-update) | async-done | bytes 2097168 | tf_op jit(solution)/shard_map/all_gather | solution.py:70
  105.8 2.2 multiply_subtract_fusion.10
  108.3 2.4 fusion.1
  113.1 2.3 fusion.3
  117.1 2.3 multiply_subtract_fusion.8
  119.5 15.7 %collective-permute-done = f32[2,512,128]{2,1,0:T(8,128)} collective-permute-done((f32[2,512,128]{2,1,0:T(8,128)}, f32[2,512,128]{2,1,0:T(8,128)}, u32[]{:S(2)}, u32[]{:S(2)}) %collective-permute-start) | collective-permute-done | bytes 524320 | tf_op jit(solution)/shard_map/ppermute | solution.py:18
  135.8 3.7 %multiply_reduce_fusion.2 = (f32[]{:T(128)}, bf16[2048,512]{1,0:T(8,128)(2,1)S(1)}) fusion(f32[256,8,4,128]{3,2,1,0:T(4,128)S(1)} %bitcast.200, bf16[4,2048,512]{2,1,0:T(8,128)(2,1)} %param.7, f32[2,512,128]{2,1,0:T(8,128)} %collective-permute-done, f32[2048,128]{1,0:T(8,128)S(1)} %get-tuple-element.33), kind=kOutput, calls=%fused_computation.34 | convolution fusion | flops 274989056 | bytes 9568260 | tf_op jit(solution)/shard_map/dot_general | solution.py:25
  139.5 1.9 multiply_subtract_fusion.17
  151.4 1.9 multiply_subtract_fusion.5
  153.3 14.0 %collective-permute-done.1 = f32[2,512,128]{2,1,0:T(8,128)} collective-permute-done((f32[2,512,128]{2,1,0:T(8,128)}, f32[2,512,128]{2,1,0:T(8,128)}, u32[]{:S(2)}, u32[]{:S(2)}) %collective-permute-start.1) | collective-permute-done | bytes 524320 | tf_op jit(solution)/shard_map/ppermute | solution.py:18
  167.9 3.7 %multiply_reduce_fusion.1 = (f32[]{:T(128)}, bf16[2048,512]{1,0:T(8,128)(2,1)S(1)}) fusion(f32[256,8,4,128]{3,2,1,0:T(4,128)S(1)} %bitcast.203, bf16[4,2048,512]{2,1,0:T(8,128)(2,1)} %param.7, f32[2,512,128]{2,1,0:T(8,128)} %collective-permute-done.1, f32[2048,128]{1,0:T(8,128)S(1)} %get-tuple-element.69), kind=kOutput, calls=%fused_computation.33 | convolution fusion | flops 274989056 | bytes 9568260 | tf_op jit(solution)/shard_map/dot_general | solution.py:25
  171.6 1.9 multiply_subtract_fusion.15
  183.2 2.3 multiply_subtract_fusion.2
  185.5 12.7 %collective-permute-done.2 = f32[2,512,128]{2,1,0:T(8,128)} collective-permute-done((f32[2,512,128]{2,1,0:T(8,128)}, f32[2,512,128]{2,1,0:T(8,128)}, u32[]{:S(2)}, u32[]{:S(2)}) %collective-permute-start.2) | collective-permute-done | bytes 524320 | tf_op jit(solution)/shard_map/ppermute | solution.py:18
  198.8 3.7 %multiply_reduce_fusion = (f32[]{:T(128)}, bf16[2048,512]{1,0:T(8,128)(2,1)S(1)}) fusion(f32[256,8,4,128]{3,2,1,0:T(4,128)S(1)} %bitcast.206, bf16[4,2048,512]{2,1,0:T(8,128)(2,1)} %param.7, f32[2,512,128]{2,1,0:T(8,128)} %collective-permute-done.2, f32[2048,128]{1,0:T(8,128)S(1)} %get-tuple-element.27), kind=kOutput, calls=%fused_computation.32 | convolution fusion | flops 274989056 | bytes 9568260 | tf_op jit(solution)/shard_map/dot_general | solution.py:25
  202.5 1.9 multiply_subtract_fusion.13
  204.4 1.8 multiply_subtract_fusion.1
  207.7 2.4 multiply_subtract_fusion.12
  215.5 3.1 slice.88
  221.2 41.4 %all-reduce = (f32[]{:T(128)}, f32[]{:T(128)}, f32[]{:T(128)}, f32[]{:T(128)}, f32[]{:T(128)}, /*index=5*/f32[]{:T(128)}, f32[]{:T(128)}, f32[]{:T(128)}) all-reduce(f32[]{:T(128)} %get-tuple-element.45, f32[]{:T(128)S(6)} %mul.689, f32[]{:T(128)} %get-tuple-element.43, ...), channel_id=1, replica_groups=mesh['row'=8,'col'=4] {'row','col'}, use_global_device_ids=true, to_apply=%region_17.18 | all-reduce | flops 8 | bytes 64 | tf_op jit(solution)/shard_map/psum | solution.py:89
  268.4 2.6 multiply_subtract_fusion.11
  271.1 31.3 %reduce-scatter.3.cloned.1.call-done = f32[1024,128]{1,0:T(8,128)} async-done(((f32[4096,128]{1,0:T(8,128)}), f32[1024,128]{1,0:T(8,128)}) %reduce-scatter.3.cloned.1.call-update) | async-done | bytes 524304 | tf_op jit(solution)/shard_map/reduce_scatter | solution.py:106
  (101 shorter events, 44.6 us)
Async XLA Ops:
  7.2 51.1 %all-gather.3.cloned.1.call-start = ((), (), s32[]{:S(2)}) async-start(), calls=%async_computation.2 | async-start | bytes 2621440 | tf_op jit(solution)/shard_map/all_gather | solution.py:69
  7.9 96.6 %all-gather.5.cloned.1.call-start = ((), (), s32[]{:S(2)}) async-start(), calls=%async_computation.3 | async-start | bytes 2621440 | tf_op jit(solution)/shard_map/all_gather | solution.py:70
  8.6 262.4 %reduce-scatter.5.cloned.1.call-start = ((), (), s32[]{:S(2)}) async-start(), calls=%async_computation.5 | async-start | bytes 2621440 | tf_op jit(solution)/shard_map/reduce_scatter | solution.py:109
  61.7 5.0 %copy-start = (f32[16,128,4,128]{3,2,1,0:T(4,128)}, f32[16,128,4,128]{3,2,1,0:T(4,128)S(1)}, u32[]{:S(2)}) copy-start(f32[16,128,4,128]{3,2,1,0:T(4,128)S(1)} %mul.539) | copy-start | bytes 12582916
  62.1 4.7 %copy-start.10 = (f32[512,128]{1,0:T(8,128)S(1)}, f32[512,128]{1,0:T(8,128)}, u32[]{:S(2)}) copy-start(f32[512,128]{1,0:T(8,128)} %param.13) | copy-start | bytes 786436
  104.5 1.3 copy-start.9
  105.8 2.5 copy-start.1
  108.0 3.5 %copy-start.2 = (f32[2048,128]{1,0:T(8,128)}, f32[2048,128]{1,0:T(8,128)S(1)}, u32[]{:S(2)}) copy-start(f32[2048,128]{1,0:T(8,128)S(1)} %get-tuple-element.38) | copy-start | bytes 3145732
  108.3 2.4 copy-start.11
  108.3 2.4 copy-start.12
  111.4 4.0 %copy-start.6 = (f32[512,128]{1,0:T(8,128)}, f32[512,128]{1,0:T(8,128)S(1)}, u32[]{:S(2)}) copy-start(f32[512,128]{1,0:T(8,128)S(1)} %get-tuple-element.35) | copy-start | bytes 786436
  117.0 18.1 %collective-permute-start = (f32[2,512,128]{2,1,0:T(8,128)}, f32[2,512,128]{2,1,0:T(8,128)}, u32[]{:S(2)}, u32[]{:S(2)}) collective-permute-start(f32[2,512,128]{2,1,0:T(8,128)} %pad_maximum_fusion), channel_id=1, source_target_pairs={{0,1},{1,2},{2,3},{3,4},{4,5},{5,6},{6,7},{7,8},{8,9},{9,10},{10,1... | collective-permute-start | bytes 1572872 | tf_op jit(solution)/shard_map/ppermute | solution.py:18
  135.8 7.4 %slice-start = ((s8[8388608]{0:T(1024)(128)(4,1)}), s8[4194304]{0:T(1024)(128)(4,1)S(1)}, s32[]{:S(2)}) async-start(s8[8388608]{0:T(1024)(128)(4,1)} %bitcast.191), calls=%async_computation.6 | async-start | bytes 8388608
  139.5 3.6 %slice-start.1 = ((s8[8388608]{0:T(1024)(128)(4,1)}), s8[4194304]{0:T(1024)(128)(4,1)S(1)}, s32[]{:S(2)}) async-start(s8[8388608]{0:T(1024)(128)(4,1)} %bitcast.191), calls=%async_computation.7 | async-start | bytes 8388608
  150.7 16.7 %collective-permute-start.1 = (f32[2,512,128]{2,1,0:T(8,128)}, f32[2,512,128]{2,1,0:T(8,128)}, u32[]{:S(2)}, u32[]{:S(2)}) collective-permute-start(f32[2,512,128]{2,1,0:T(8,128)} %pad_maximum_fusion.1), channel_id=1, source_target_pairs={{0,1},{1,2},{2,3},{3,4},{4,5},{5,6},{6,7},{7,8},{8,9},{9,10},{10,1... | collective-permute-start | bytes 1572872 | tf_op jit(solution)/shard_map/ppermute | solution.py:18
  167.9 7.4 %slice-start.2 = ((s8[8388608]{0:T(1024)(128)(4,1)}), s8[4194304]{0:T(1024)(128)(4,1)S(1)}, s32[]{:S(2)}) async-start(s8[8388608]{0:T(1024)(128)(4,1)} %bitcast.193), calls=%async_computation.8 | async-start | bytes 8388608
  171.6 1.9 copy-start.3
  171.6 3.7 %slice-start.3 = ((s8[8388608]{0:T(1024)(128)(4,1)}), s8[4194304]{0:T(1024)(128)(4,1)S(1)}, s32[]{:S(2)}) async-start(s8[8388608]{0:T(1024)(128)(4,1)} %bitcast.193), calls=%async_computation.9 | async-start | bytes 8388608
  183.0 15.1 %collective-permute-start.2 = (f32[2,512,128]{2,1,0:T(8,128)}, f32[2,512,128]{2,1,0:T(8,128)}, u32[]{:S(2)}, u32[]{:S(2)}) collective-permute-start(f32[2,512,128]{2,1,0:T(8,128)} %pad_maximum_fusion.2), channel_id=1, source_target_pairs={{0,1},{1,2},{2,3},{3,4},{4,5},{5,6},{6,7},{7,8},{8,9},{9,10},{10,1... | collective-permute-start | bytes 1572872 | tf_op jit(solution)/shard_map/ppermute | solution.py:18
  198.7 7.5 %slice-start.4 = ((s8[8388608]{0:T(1024)(128)(4,1)}), s8[4194304]{0:T(1024)(128)(4,1)S(1)}, s32[]{:S(2)}) async-start(s8[8388608]{0:T(1024)(128)(4,1)} %bitcast.195), calls=%async_computation.10 | async-start | bytes 8388608
  202.5 3.7 %slice-start.5 = ((s8[8388608]{0:T(1024)(128)(4,1)}), s8[4194304]{0:T(1024)(128)(4,1)S(1)}, s32[]{:S(2)}) async-start(s8[8388608]{0:T(1024)(128)(4,1)} %bitcast.195), calls=%async_computation.11 | async-start | bytes 8388608
  204.4 3.3 %copy-start.7 = (f32[512,128]{1,0:T(8,128)}, f32[512,128]{1,0:T(8,128)S(1)}, u32[]{:S(2)}) copy-start(f32[512,128]{1,0:T(8,128)S(1)} %get-tuple-element.80) | copy-start | bytes 786436
  211.8 1.6 copy-start.5
  215.4 86.9 %reduce-scatter.3.cloned.1.call-start = ((), (), s32[]{:S(2)}) async-start(), calls=%async_computation.4 | async-start | bytes 2621440 | tf_op jit(solution)/shard_map/reduce_scatter | solution.py:106
  (4 other events, 4.4 us)
Sparse Core Ops, SparseCore 0:
  9.6 48.6 all-gather.2
  59.8 44.6 all-gather.4
  215.6 40.7 reduce-scatter.4
  259.2 43.1 reduce-scatter.2
where the time goes:
time: 310 us; the launch traced here: 309 us
  waiting for transfers between devices  157 us (51%)
  matrix products  64 us (21%)
  blocking collectives  41.4 us (13%)
  between operations  22.7 us (7%)
  local copies, waits for them, and re-layouts  12.8 us (4%)
  other arithmetic  11.2 us (4%)
    all_gather x1, waiting for transfers between devices, on_device(): lax.all_gather(users, 'col', axis=0, tiled=True)  45.4 us
    ppermute x3, waiting for transfers between devices, passed_along(): return lax.ppermute(value, axis, pairs)  42.3 us
    psum x1, blocking collectives, on_device(): total_error, total_count = lax.psum((sq_error, observed), ('row', 'col'))  41.4 us
    all_gather x1, waiting for transfers between devices, on_device(): lax.all_gather(user_accum, 'col', axis=0, tiled=True)  36.3 us
    reduce_scatter x1, waiting for transfers between devices, on_device(): lax.psum_scatter(frame_fac[:group_size * arrived_rows], 'col', scatter_di...  31.3 us
    dot_general x12, matrix products, update(): lax.dot_general(user_half, item_half, (((1,), (1,)), ((), ())), preferred...  24.8 us
    dot_general x12, matrix products, update(): jnp.dot(err_half, item_half, preferred_element_type=jnp.float32)  20.4 us
    dot_general x12, matrix products, update(): lax.dot_general(err_half, user_half, (((0,), (0,)), ((), ())), preferred_...  18.7 us
  transfers between devices with their start and end apart: 7, of which 6 were waited for; matrix products, arithmetic and copies ran while one was open for 8% of the time, Pallas kernels for 0%

commit v1 on v0

--- a/solution.py
+++ b/solution.py
@@ -51,6 +51,53 @@
     return (user_fac, user_acc, item_fac, item_acc, sq_error)
 
 
+def segment_plan(group_size, own_tiles):
+    total = group_size * own_tiles
+    low = [m if m < group_size - 1 else total - 2 * own_tiles for m in range(group_size)]
+    high = [total - (group_size - 1 - m) if m else 2 * own_tiles for m in range(group_size)]
+    segments = []
+    for step in range(1 - group_size, group_size):
+        first, last, pairs = own_tiles, 0, []
+        for m in range(group_size):
+            home = m + step
+            if 0 <= home < group_size:
+                begin = max(low[m], home * own_tiles) - home * own_tiles
+                end = min(high[m], (home + 1) * own_tiles) - home * own_tiles
+                if begin < end:
+                    first, last = min(first, begin), max(last, end)
+                    pairs.append((home, m))
+        if step == 0:
+            first, last = 0, own_tiles
+        if pairs:
+            segments.append((step, first, last, pairs))
+    return segments
+
+
+def fetched(own, segments, tile_size, window, rows):
+    parts = []
+    for step, first, last, pairs in segments:
+        part = own[first * tile_size : last * tile_size]
+        parts.append(lax.ppermute(part, "col", pairs) if step else part)
+    parts.append(jnp.zeros((rows, own.shape[1]), own.dtype))
+    return lax.dynamic_slice_in_dim(jnp.concatenate(parts, axis=0), window, rows, 0)
+
+
+def returned(kept, segments, tile_size, window):
+    lengths = [(last - first) * tile_size for step, first, last, pairs in segments]
+    frame = jnp.zeros((sum(lengths) + kept.shape[0], kept.shape[1]), kept.dtype)
+    frame = lax.dynamic_update_slice_in_dim(frame, kept, window, 0)
+    own_rows = [length for length, segment in zip(lengths, segments) if segment[0] == 0][0]
+    total, at = None, 0
+    for length, (step, first, last, pairs) in zip(lengths, segments):
+        part = frame[at : at + length]
+        at += length
+        if step:
+            part = lax.ppermute(part, "col", [(m, home) for home, m in pairs])
+        part = jnp.pad(part, ((first * tile_size, own_rows - last * tile_size), (0, 0)))
+        total = part if total is None else total + part
+    return total
+
+
 def on_device(ratings, tile_mask, tile_counts, users, user_accum, items, item_accum):
     strata_count = ratings.shape[0]
     slot_count = tile_mask.shape[1]
@@ -65,15 +112,13 @@
     start_tile = jnp.sum(jnp.where(ranks < member, group_counts, 0))
     own_count = jnp.sum(jnp.where(ranks == member, group_counts, 0))
     valid = (jnp.arange(slot_count, dtype=jnp.int32) < own_count).astype(jnp.float32)
-    whole_fac, whole_acc = (
-        lax.all_gather(users, "col", axis=0, tiled=True),
-        lax.all_gather(user_accum, "col", axis=0, tiled=True),
-    )
     pad_rows = slot_count * tile_size
-    ext_fac = jnp.concatenate([whole_fac, whole_fac[:pad_rows]], axis=0)
-    ext_acc = jnp.concatenate([whole_acc, whole_acc[:pad_rows]], axis=0)
-    user_fac = lax.dynamic_slice_in_dim(ext_fac, start_tile * tile_size, pad_rows, 0)
-    user_acc = lax.dynamic_slice_in_dim(ext_acc, start_tile * tile_size, pad_rows, 0)
+    segments = segment_plan(group_size, arrived_rows // tile_size)
+    ahead = -min(step * (arrived_rows // tile_size) + first for step, first, last, pairs in segments)
+    window = (start_tile - member * (arrived_rows // tile_size) + ahead) * tile_size
+    row_valid = jnp.repeat(valid, tile_size)[:, None] > 0.5
+    user_fac = jnp.where(row_valid, fetched(users, segments, tile_size, window, pad_rows), 0.0)
+    user_acc = jnp.where(row_valid, fetched(user_accum, segments, tile_size, window, pad_rows), 1.0)
     held_pair = jnp.stack([items, item_accum])
     loss_list = []
     for stratum in range(strata_count):
@@ -92,24 +137,8 @@
         if stratum + 1 < strata_count:
             held_pair = passed_along(held_pair, ("row", "col"), 1)
     losses = jnp.stack(loss_list)
-    row_valid = jnp.repeat(valid, tile_size)[:, None] > 0.5
-    kept_fac = jnp.where(row_valid, user_fac, 0.0)
-    kept_acc = jnp.where(row_valid, user_acc, 0.0)
-    frame_rows = group_size * arrived_rows + pad_rows
-    frame_fac = lax.dynamic_update_slice_in_dim(
-        jnp.zeros((frame_rows, kept_fac.shape[1]), jnp.float32), kept_fac, start_tile * tile_size, 0
-    )
-    frame_acc = lax.dynamic_update_slice_in_dim(
-        jnp.zeros((frame_rows, kept_acc.shape[1]), jnp.float32), kept_acc, start_tile * tile_size, 0
-    )
-    users_new, accum_new = (
-        lax.psum_scatter(
-            frame_fac[: group_size * arrived_rows], "col", scatter_dimension=0, tiled=True
-        ),
-        lax.psum_scatter(
-            frame_acc[: group_size * arrived_rows], "col", scatter_dimension=0, tiled=True
-        ),
-    )
+    users_new = returned(jnp.where(row_valid, user_fac, 0.0), segments, tile_size, window)
+    accum_new = returned(jnp.where(row_valid, user_acc, 0.0), segments, tile_size, window)
     return (users_new, accum_new, held_pair[0], held_pair[1], losses)
 
 

time: 310 us -> 248 us (0.80)
  waiting for transfers between devices: 157 us -> 58.8 us
  starting transfers between devices: 0.17 us -> 48.3 us
  between operations: 22.7 us -> 9.78 us
  matrix products: 64 us -> 55.6 us
  blocking collectives: 41.4 us -> 46.4 us
  other arithmetic: 11.2 us -> 14.4 us
    all_gather x2 -> x0, waiting for transfers between devices: 81.6 us -> none  [the longest x1 45.4 us: on_device(): lax.all_gather(users, 'col', axis=0, tiled=True)]
    ppermute x0 -> x16, starting transfers between devices: none -> 33.6 us  [the longest x8 18.9 us: fetched(): parts.append(lax.ppermute(part, 'col', pairs) if step else part)]
    reduce_scatter x2 -> x0, waiting for transfers between devices: 31.3 us -> none  [the longest x1 31.3 us: on_device(): lax.psum_scatter(frame_fac[:group_size * arrived_rows], 'col', scatter_di...]
    ppermute x0 -> x16, waiting for transfers between devices: none -> 27.6 us  [the longest x8 18 us: fetched(): parts.append(lax.ppermute(part, 'col', pairs) if step else part)]
    ppermute x3, starting transfers between devices: 0.01 us -> 14.7 us  [passed_along(): return lax.ppermute(value, axis, pairs)]
    ppermute x3, waiting for transfers between devices: 42.3 us -> 31.3 us  [passed_along(): return lax.ppermute(value, axis, pairs)]
    dot_general x12, matrix products: 24.8 us -> 19.2 us  [update(): lax.dot_general(user_half, item_half, (((1,), (1,)), ((), ())), preferred...]
    psum x1, blocking collectives: 41.4 us -> 46.4 us  [on_device(): total_error, total_count = lax.psum((sq_error, observed), ('row', 'col'))]
  transfers between devices with their start and end apart: 7 -> 19, of which waited for: 6 -> 6; matrix products, arithmetic and copies ran while one was open for 8% -> 9% of each run, Pallas kernels for 0% -> 0%
where the time goes in v1:
time: 248 us; the launch traced here: 246 us
  waiting for transfers between devices  58.8 us (24%)
  matrix products  55.6 us (22%)
  starting transfers between devices  48.3 us (19%)
  blocking collectives  46.4 us (19%)
  other arithmetic  14.4 us (6%)
  local copies, waits for them, and re-layouts  13.1 us (5%)
  between operations  9.78 us (4%)
    psum x1, blocking collectives, on_device(): total_error, total_count = lax.psum((sq_error, observed), ('row', 'col'))  46.4 us
    ppermute x3, waiting for transfers between devices, passed_along(): return lax.ppermute(value, axis, pairs)  31.3 us
    dot_general x12, matrix products, update(): lax.dot_general(user_half, item_half, (((1,), (1,)), ((), ())), preferred...  19.2 us
    ppermute x8, starting transfers between devices, fetched(): parts.append(lax.ppermute(part, 'col', pairs) if step else part)  18.9 us
    dot_general x12, matrix products, update(): jnp.dot(err_half, item_half, preferred_element_type=jnp.float32)  18.9 us
    ppermute x8, waiting for transfers between devices, fetched(): parts.append(lax.ppermute(part, 'col', pairs) if step else part)  18 us
    dot_general x12, matrix products, update(): lax.dot_general(err_half, user_half, (((0,), (0,)), ((), ())), preferred_...  17.6 us
    ppermute x8, starting transfers between devices, returned(): part = lax.ppermute(part, 'col', [(m, home) for home, m in pairs])  14.7 us
  transfers between devices with their start and end apart: 19, of which 6 were waited for; matrix products, arithmetic and copies ran while one was open for 9% of the time, Pallas kernels for 0%

profile of v1, /device:TPU:0, one launch (start us, length us, event | category | flops | bytes accessed | tf_op | source)
XLA Modules:
  0.0 246.5 jit_solution(2244958160504731430)
XLA Ops:
  0.6 5.1 %collective-permute-start.1 = (f32[1024,128]{1,0:T(8,128)}, f32[1024,128]{1,0:T(8,128)S(1)}, u32[]{:S(2)}, u32[]{:S(2)}) collective-permute-start(f32[1024,128]{1,0:T(8,128)} %param.10), channel_id=1, source_target_pairs={{0,1},{1,2},{2,3},{4,5},{5,6},{6,7},{8,9},{9,10},{10,11},{12,13},{... | collective-permute-start | bytes 1572872 | tf_op jit(solution)/shard_map/ppermute | solution.py:80
  7.0 2.0 fusion.125
  9.1 5.7 %collective-permute-start = (f32[768,128]{1,0:T(8,128)}, f32[768,128]{1,0:T(8,128)S(1)}, u32[]{:S(2)}, u32[]{:S(2)}) collective-permute-start(f32[768,128]{1,0:T(8,128)} %get-tuple-element.64), channel_id=1, source_target_pairs={{0,2},{4,6},{8,10},{12,14},{16,18},{20,22},{24,26},{28,30}} | collective-permute-start | bytes 1179656 | tf_op jit(solution)/shard_map/ppermute | solution.py:80
  16.1 2.1 fusion.124
  18.2 2.9 %collective-permute-start.4 = (f32[768,128]{1,0:T(8,128)}, f32[768,128]{1,0:T(8,128)S(1)}, u32[]{:S(2)}, u32[]{:S(2)}) collective-permute-start(f32[768,128]{1,0:T(8,128)} %get-tuple-element.62), channel_id=1, source_target_pairs={{0,2},{4,6},{8,10},{12,14},{16,18},{20,22},{24,26},{28,30}} | collective-permute-start | bytes 1179656 | tf_op jit(solution)/shard_map/ppermute | solution.py:80
  28.1 17.2 %collective-permute-done.4 = f32[768,128]{1,0:T(8,128)S(1)} collective-permute-done((f32[768,128]{1,0:T(8,128)}, f32[768,128]{1,0:T(8,128)S(1)}, u32[]{:S(2)}, u32[]{:S(2)}) %collective-permute-start.4) | collective-permute-done | bytes 393248 | tf_op jit(solution)/shard_map/ppermute | solution.py:80
  49.3 2.4 multiply_reduce_fusion.3
  59.3 12.2 %collective-permute-start.8 = (f32[2,512,128]{2,1,0:T(8,128)}, f32[2,512,128]{2,1,0:T(8,128)}, u32[]{:S(2)}, u32[]{:S(2)}) collective-permute-start(f32[2,512,128]{2,1,0:T(8,128)} %pad_maximum_fusion), channel_id=1, source_target_pairs={{0,1},{1,2},{2,3},{3,4},{4,5},{5,6},{6,7},{7,8},{8,9},{9,10},{10,1... | collective-permute-start | bytes 1572872 | tf_op jit(solution)/shard_map/ppermute | solution.py:18
  71.5 2.3 multiply_subtract_fusion.8
  73.8 6.2 %collective-permute-done.8 = f32[2,512,128]{2,1,0:T(8,128)} collective-permute-done((f32[2,512,128]{2,1,0:T(8,128)}, f32[2,512,128]{2,1,0:T(8,128)}, u32[]{:S(2)}, u32[]{:S(2)}) %collective-permute-start.8) | collective-permute-done | bytes 524320 | tf_op jit(solution)/shard_map/ppermute | solution.py:18
  80.6 3.7 %multiply_reduce_fusion.2 = (f32[]{:T(128)}, bf16[2048,512]{1,0:T(8,128)(2,1)S(1)}) fusion(f32[256,8,4,128]{3,2,1,0:T(4,128)S(1)} %bitcast.199, bf16[4,2048,512]{2,1,0:T(8,128)(2,1)} %param.7, f32[2,512,128]{2,1,0:T(8,128)} %collective-permute-done.8, f32[2048,128]{1,0:T(8,128)S(1)} %get-tuple-element.33), kind=kOutput, calls=%fused_computation.34 | convolution fusion | flops 274989056 | bytes 9568260 | tf_op jit(solution)/shard_map/dot_general | solution.py:25
  95.5 2.5 %collective-permute-start.9 = (f32[2,512,128]{2,1,0:T(8,128)}, f32[2,512,128]{2,1,0:T(8,128)}, u32[]{:S(2)}, u32[]{:S(2)}) collective-permute-start(f32[2,512,128]{2,1,0:T(8,128)} %pad_maximum_fusion.1), channel_id=1, source_target_pairs={{0,1},{1,2},{2,3},{3,4},{4,5},{5,6},{6,7},{7,8},{8,9},{9,10},{10,1... | collective-permute-start | bytes 1572872 | tf_op jit(solution)/shard_map/ppermute | solution.py:18
  100.0 13.5 %collective-permute-done.9 = f32[2,512,128]{2,1,0:T(8,128)} collective-permute-done((f32[2,512,128]{2,1,0:T(8,128)}, f32[2,512,128]{2,1,0:T(8,128)}, u32[]{:S(2)}, u32[]{:S(2)}) %collective-permute-start.9) | collective-permute-done | bytes 524320 | tf_op jit(solution)/shard_map/ppermute | solution.py:18
  114.1 3.8 %multiply_reduce_fusion.1 = (f32[]{:T(128)}, bf16[2048,512]{1,0:T(8,128)(2,1)S(1)}) fusion(f32[256,8,4,128]{3,2,1,0:T(4,128)S(1)} %bitcast.202, bf16[4,2048,512]{2,1,0:T(8,128)(2,1)} %param.7, f32[2,512,128]{2,1,0:T(8,128)} %collective-permute-done.9, f32[2048,128]{1,0:T(8,128)S(1)} %get-tuple-element.81), kind=kOutput, calls=%fused_computation.33 | convolution fusion | flops 274989056 | bytes 9568260 | tf_op jit(solution)/shard_map/dot_general | solution.py:25
  132.0 2.3 multiply_subtract_fusion.2
  134.3 11.6 %collective-permute-done.10 = f32[2,512,128]{2,1,0:T(8,128)} collective-permute-done((f32[2,512,128]{2,1,0:T(8,128)}, f32[2,512,128]{2,1,0:T(8,128)}, u32[]{:S(2)}, u32[]{:S(2)}) %collective-permute-start.10) | collective-permute-done | bytes 524320 | tf_op jit(solution)/shard_map/ppermute | solution.py:18
  146.5 3.7 %multiply_reduce_fusion = (f32[]{:T(128)}, bf16[2048,512]{1,0:T(8,128)(2,1)S(1)}) fusion(f32[256,8,4,128]{3,2,1,0:T(4,128)S(1)} %bitcast.205, bf16[4,2048,512]{2,1,0:T(8,128)(2,1)} %param.7, f32[2,512,128]{2,1,0:T(8,128)} %collective-permute-done.10, f32[2048,128]{1,0:T(8,128)S(1)} %get-tuple-element.27), kind=kOutput, calls=%fused_computation.32 | convolution fusion | flops 274989056 | bytes 9568260 | tf_op jit(solution)/shard_map/dot_general | solution.py:25
  161.9 5.4 %collective-permute-start.17 = (f32[1024,128]{1,0:T(8,128)}, f32[1024,128]{1,0:T(8,128)}, u32[]{:S(2)}, u32[]{:S(2)}) collective-permute-start(f32[1024,128]{1,0:T(8,128)} %get-tuple-element.50), channel_id=1, source_target_pairs={{0,1},{1,2},{2,3},{4,5},{5,6},{6,7},{8,9},{9,10},{10,11},{12,13},{... | collective-permute-start | bytes 1572872 | tf_op jit(solution)/shard_map/ppermute | solution.py:95
  172.5 9.6 %collective-permute-done.15 = f32[768,128]{1,0:T(8,128)S(1)} collective-permute-done((f32[768,128]{1,0:T(8,128)S(1)}, f32[768,128]{1,0:T(8,128)S(1)}, u32[]{:S(2)}, u32[]{:S(2)}) %collective-permute-start.15) | collective-permute-done | bytes 393248 | tf_op jit(solution)/shard_map/ppermute | solution.py:95
  182.1 2.1 collective-permute-start.13
  187.0 2.5 %multiply_subtract_fusion.11 = (f32[512,128]{1,0:T(8,128)}, f32[512,128]{1,0:T(8,128)}) fusion(f32[512,128]{1,0:T(8,128)S(1)} %get-tuple-element.93, f32[512,128]{1,0:T(8,128)S(1)} %get-tuple-element.94, f32[512,128]{1,0:T(8,128)S(1)} %get-tuple-element.92, f32[2,512,128]{2,1,0:T(8,128)} %collective-permute-done.10, bf16[2048,512]{1,0:T(8,128)(2,1)S(1)} %fusion.15, ...), kind=kOutput, calls=%fused_computation.126 | convolution fusion | flops 269484032 | bytes 4718592 | tf_op jit(solution)/shard_map/dot_general | solution.py:41
  189.5 46.4 %all-reduce.4 = (f32[]{:T(128)}, f32[]{:T(128)}, f32[]{:T(128)}, f32[]{:T(128)}, f32[]{:T(128)}, /*index=5*/f32[]{:T(128)}, f32[]{:T(128)}, f32[]{:T(128)}) all-reduce(f32[]{:T(128)} %get-tuple-element.45, f32[]{:T(128)S(6)} %mul.690, f32[]{:T(128)} %get-tuple-element.43, ...), channel_id=1, replica_groups=mesh['row'=8,'col'=4] {'row','col'}, use_global_device_ids=true, to_apply=%region_15.16 | all-reduce | flops 8 | bytes 64 | tf_op jit(solution)/shard_map/psum | solution.py:134
  241.6 2.3 fusion.36
  244.0 2.5 %fusion.38 = f32[1024,128]{1,0:T(8,128)} fusion(f32[1024,128]{1,0:T(8,128)} %collective-permute-done.13, f32[6656,128]{1,0:T(8,128)} %copy-done, f32[768,128]{1,0:T(8,128)} %collective-permute-done.14, f32[1024,128]{1,0:T(8,128)} %collective-permute-done.12, f32[768,128]{1,0:T(8,128)} %collective-permute-done.11), kind=kLoop, calls=%fused_computation.111 | loop fusion | flops 524288 | bytes 2883584 | tf_op jit(solution)/shard_map/add | solution.py:97
  (135 shorter events, 67.0 us)
Async XLA Ops:
  0.6 46.2 %copy-start.4 = (f32[1024,128]{1,0:T(8,128)S(1)}, f32[1024,128]{1,0:T(8,128)}, u32[]{:S(2)}) copy-start(f32[1024,128]{1,0:T(8,128)} %param.10) | copy-start | bytes 1572868
  0.6 45.4 %collective-permute-start.1 = (f32[1024,128]{1,0:T(8,128)}, f32[1024,128]{1,0:T(8,128)S(1)}, u32[]{:S(2)}, u32[]{:S(2)}) collective-permute-start(f32[1024,128]{1,0:T(8,128)} %param.10), channel_id=1, source_target_pairs={{0,1},{1,2},{2,3},{4,5},{5,6},{6,7},{8,9},{9,10},{10,11},{12,13},{... | collective-permute-start | bytes 1572872 | tf_op jit(solution)/shard_map/ppermute | solution.py:80
  5.7 41.2 %collective-permute-start.2 = (f32[1024,128]{1,0:T(8,128)}, f32[1024,128]{1,0:T(8,128)S(1)}, u32[]{:S(2)}, u32[]{:S(2)}) collective-permute-start(f32[1024,128]{1,0:T(8,128)} %param.10), channel_id=1, source_target_pairs={{1,0},{2,1},{3,2},{5,4},{6,5},{7,6},{9,8},{10,9},{11,10},{13,12},{... | collective-permute-start | bytes 1572872 | tf_op jit(solution)/shard_map/ppermute | solution.py:80
  9.1 37.8 %copy-start.5 = (f32[1024,128]{1,0:T(8,128)S(1)}, f32[1024,128]{1,0:T(8,128)}, u32[]{:S(2)}) copy-start(f32[1024,128]{1,0:T(8,128)} %param.11) | copy-start | bytes 1572868
  9.1 17.7 %collective-permute-start = (f32[768,128]{1,0:T(8,128)}, f32[768,128]{1,0:T(8,128)S(1)}, u32[]{:S(2)}, u32[]{:S(2)}) collective-permute-start(f32[768,128]{1,0:T(8,128)} %get-tuple-element.64), channel_id=1, source_target_pairs={{0,2},{4,6},{8,10},{12,14},{16,18},{20,22},{24,26},{28,30}} | collective-permute-start | bytes 1179656 | tf_op jit(solution)/shard_map/ppermute | solution.py:80
  14.8 32.1 %collective-permute-start.5 = (f32[1024,128]{1,0:T(8,128)}, f32[1024,128]{1,0:T(8,128)S(1)}, u32[]{:S(2)}, u32[]{:S(2)}) collective-permute-start(f32[1024,128]{1,0:T(8,128)} %param.11), channel_id=1, source_target_pairs={{0,1},{1,2},{2,3},{4,5},{5,6},{6,7},{8,9},{9,10},{10,11},{12,13},{... | collective-permute-start | bytes 1572872 | tf_op jit(solution)/shard_map/ppermute | solution.py:80
  18.2 27.1 %collective-permute-start.4 = (f32[768,128]{1,0:T(8,128)}, f32[768,128]{1,0:T(8,128)S(1)}, u32[]{:S(2)}, u32[]{:S(2)}) collective-permute-start(f32[768,128]{1,0:T(8,128)} %get-tuple-element.62), channel_id=1, source_target_pairs={{0,2},{4,6},{8,10},{12,14},{16,18},{20,22},{24,26},{28,30}} | collective-permute-start | bytes 1179656 | tf_op jit(solution)/shard_map/ppermute | solution.py:80
  26.8 20.3 %collective-permute-start.6 = (f32[1024,128]{1,0:T(8,128)}, f32[1024,128]{1,0:T(8,128)S(1)}, u32[]{:S(2)}, u32[]{:S(2)}) collective-permute-start(f32[1024,128]{1,0:T(8,128)} %param.11), channel_id=1, source_target_pairs={{1,0},{2,1},{3,2},{5,4},{6,5},{7,6},{9,8},{10,9},{11,10},{13,12},{... | collective-permute-start | bytes 1572872 | tf_op jit(solution)/shard_map/ppermute | solution.py:80
  28.1 19.9 %slice-start = ((s8[8388608]{0:T(1024)(128)(4,1)}), s8[4194304]{0:T(1024)(128)(4,1)S(1)}, s32[]{:S(2)}) async-start(s8[8388608]{0:T(1024)(128)(4,1)} %bitcast.191), calls=%async_computation | async-start | bytes 8388608
  45.3 1.7 collective-permute-start.3
  46.1 1.2 collective-permute-start.7
  59.3 20.7 %collective-permute-start.8 = (f32[2,512,128]{2,1,0:T(8,128)}, f32[2,512,128]{2,1,0:T(8,128)}, u32[]{:S(2)}, u32[]{:S(2)}) collective-permute-start(f32[2,512,128]{2,1,0:T(8,128)} %pad_maximum_fusion), channel_id=1, source_target_pairs={{0,1},{1,2},{2,3},{3,4},{4,5},{5,6},{6,7},{7,8},{8,9},{9,10},{10,1... | collective-permute-start | bytes 1572872 | tf_op jit(solution)/shard_map/ppermute | solution.py:18
  95.5 18.0 %collective-permute-start.9 = (f32[2,512,128]{2,1,0:T(8,128)}, f32[2,512,128]{2,1,0:T(8,128)}, u32[]{:S(2)}, u32[]{:S(2)}) collective-permute-start(f32[2,512,128]{2,1,0:T(8,128)} %pad_maximum_fusion.1), channel_id=1, source_target_pairs={{0,1},{1,2},{2,3},{3,4},{4,5},{5,6},{6,7},{7,8},{8,9},{9,10},{10,1... | collective-permute-start | bytes 1572872 | tf_op jit(solution)/shard_map/ppermute | solution.py:18
  114.1 7.4 %slice-start.4 = ((s8[8388608]{0:T(1024)(128)(4,1)}), s8[4194304]{0:T(1024)(128)(4,1)S(1)}, s32[]{:S(2)}) async-start(s8[8388608]{0:T(1024)(128)(4,1)} %bitcast.195), calls=%async_computation.4 | async-start | bytes 8388608
  129.3 16.5 %collective-permute-start.10 = (f32[2,512,128]{2,1,0:T(8,128)}, f32[2,512,128]{2,1,0:T(8,128)}, u32[]{:S(2)}, u32[]{:S(2)}) collective-permute-start(f32[2,512,128]{2,1,0:T(8,128)} %pad_maximum_fusion.2), channel_id=1, source_target_pairs={{0,1},{1,2},{2,3},{3,4},{4,5},{5,6},{6,7},{7,8},{8,9},{9,10},{10,1... | collective-permute-start | bytes 1572872 | tf_op jit(solution)/shard_map/ppermute | solution.py:18
  158.6 11.6 %copy-start = (f32[6656,128]{1,0:T(8,128)}, f32[6656,128]{1,0:T(8,128)S(1)}, u32[]{:S(2)}) copy-start(f32[6656,128]{1,0:T(8,128)S(1)} %get-tuple-element.95) | copy-start | bytes 10223620
  160.6 24.9 %collective-permute-start.16 = (f32[1024,128]{1,0:T(8,128)S(1)}, f32[1024,128]{1,0:T(8,128)S(1)}, u32[]{:S(2)}, u32[]{:S(2)}) collective-permute-start(f32[1024,128]{1,0:T(8,128)S(1)} %get-tuple-element.49), channel_id=1, source_target_pairs={{1,0},{2,1},{3,2},{5,4},{6,5},{7,6},{9,8},{10,9},{11,10},{13,12},{... | collective-permute-start | bytes 1572872 | tf_op jit(solution)/shard_map/ppermute | solution.py:95
  161.9 79.7 %collective-permute-start.17 = (f32[1024,128]{1,0:T(8,128)}, f32[1024,128]{1,0:T(8,128)}, u32[]{:S(2)}, u32[]{:S(2)}) collective-permute-start(f32[1024,128]{1,0:T(8,128)} %get-tuple-element.50), channel_id=1, source_target_pairs={{0,1},{1,2},{2,3},{4,5},{5,6},{6,7},{8,9},{9,10},{10,11},{12,13},{... | collective-permute-start | bytes 1572872 | tf_op jit(solution)/shard_map/ppermute | solution.py:95
  167.3 14.8 %collective-permute-start.15 = (f32[768,128]{1,0:T(8,128)S(1)}, f32[768,128]{1,0:T(8,128)S(1)}, u32[]{:S(2)}, u32[]{:S(2)}) collective-permute-start(f32[768,128]{1,0:T(8,128)S(1)} %get-tuple-element.47), channel_id=1, source_target_pairs={{2,0},{6,4},{10,8},{14,12},{18,16},{22,20},{26,24},{30,28}} | collective-permute-start | bytes 1179656 | tf_op jit(solution)/shard_map/ppermute | solution.py:95
  168.6 15.6 %collective-permute-start.18 = (f32[768,128]{1,0:T(8,128)S(1)}, f32[768,128]{1,0:T(8,128)S(1)}, u32[]{:S(2)}, u32[]{:S(2)}) collective-permute-start(f32[768,128]{1,0:T(8,128)S(1)} %get-tuple-element.48), channel_id=1, source_target_pairs={{1,3},{5,7},{9,11},{13,15},{17,19},{21,23},{25,27},{29,31}} | collective-permute-start | bytes 1179656 | tf_op jit(solution)/shard_map/ppermute | solution.py:95
  171.2 72.7 %collective-permute-start.12 = (f32[1024,128]{1,0:T(8,128)}, f32[1024,128]{1,0:T(8,128)}, u32[]{:S(2)}, u32[]{:S(2)}) collective-permute-start(f32[1024,128]{1,0:T(8,128)} %get-tuple-element.53), channel_id=1, source_target_pairs={{1,0},{2,1},{3,2},{5,4},{6,5},{7,6},{9,8},{10,9},{11,10},{13,12},{... | collective-permute-start | bytes 1572872 | tf_op jit(solution)/shard_map/ppermute | solution.py:95
  182.1 61.9 %collective-permute-start.13 = (f32[1024,128]{1,0:T(8,128)}, f32[1024,128]{1,0:T(8,128)}, u32[]{:S(2)}, u32[]{:S(2)}) collective-permute-start(f32[1024,128]{1,0:T(8,128)} %get-tuple-element.54), channel_id=1, source_target_pairs={{0,1},{1,2},{2,3},{4,5},{5,6},{6,7},{8,9},{9,10},{10,11},{12,13},{... | collective-permute-start | bytes 1572872 | tf_op jit(solution)/shard_map/ppermute | solution.py:95
  184.2 59.7 %collective-permute-start.11 = (f32[768,128]{1,0:T(8,128)}, f32[768,128]{1,0:T(8,128)}, u32[]{:S(2)}, u32[]{:S(2)}) collective-permute-start(f32[768,128]{1,0:T(8,128)} %get-tuple-element.51), channel_id=1, source_target_pairs={{2,0},{6,4},{10,8},{14,12},{18,16},{22,20},{26,24},{30,28}} | collective-permute-start | bytes 1179656 | tf_op jit(solution)/shard_map/ppermute | solution.py:95
  185.5 58.4 %collective-permute-start.14 = (f32[768,128]{1,0:T(8,128)}, f32[768,128]{1,0:T(8,128)}, u32[]{:S(2)}, u32[]{:S(2)}) collective-permute-start(f32[768,128]{1,0:T(8,128)} %get-tuple-element.52), channel_id=1, source_target_pairs={{1,3},{5,7},{9,11},{13,15},{17,19},{21,23},{25,27},{29,31}} | collective-permute-start | bytes 1179656 | tf_op jit(solution)/shard_map/ppermute | solution.py:95
  (14 other events, 53.1 us)

commit v2 on v1

--- a/solution.py
+++ b/solution.py
@@ -1,6 +1,10 @@
+import functools
+
 import jax
 import jax.numpy as jnp
 from jax import lax
+from jax.experimental import pallas as pl
+from jax.experimental.pallas import tpu as pltpu
 from jax.sharding import PartitionSpec as P
 
 TILE = 128
@@ -18,37 +22,117 @@
     return lax.ppermute(value, axis, pairs)
 
 
-def update(user_fac, user_acc, item_fac, item_acc, rating_block, live_tiles):
-    tile_size = user_fac.shape[0] // live_tiles.shape[0]
-    user_half = user_fac.astype(jnp.bfloat16)
-    item_half = item_fac.astype(jnp.bfloat16)
-    predicted = lax.dot_general(
-        user_half, item_half, (((1,), (1,)), ((), ())), preferred_element_type=jnp.float32
-    )
-    residue = predicted - rating_block.astype(jnp.float32)
-    masked = (
-        residue.reshape(live_tiles.shape[0], tile_size, live_tiles.shape[1], tile_size)
-        * live_tiles[:, None, :, None]
-    ).reshape(residue.shape)
-    sq_error = jnp.sum(masked * residue)
-    err_half = masked.astype(jnp.bfloat16)
-    grad_user = (
-        jnp.dot(err_half, item_half, preferred_element_type=jnp.float32)
-        * float(item_fac.shape[0]) ** (-0.5)
-        + ridge_weight * user_fac
-    )
-    grad_item = (
-        lax.dot_general(
-            err_half, user_half, (((0,), (0,)), ((), ())), preferred_element_type=jnp.float32
-        )
-        * float(UT * TILE) ** (-0.5)
-        + ridge_weight * item_fac
-    )
-    user_acc = user_acc + grad_user * grad_user
-    item_acc = item_acc + grad_item * grad_item
-    user_fac = user_fac - step_rate * grad_user * lax.rsqrt(user_acc)
-    item_fac = item_fac - step_rate * grad_item * lax.rsqrt(item_acc)
-    return (user_fac, user_acc, item_fac, item_acc, sq_error)
+def stratum_kernel(
+    stratum, steps, chunks, user_scale, item_scale,
+    count_ref, live_ref, ratings_hbm, fac_in, acc_in, item_in, item_acc_in,
+    fac, acc, item, item_acc, loss_ref,
+    rating, err, item_half, item_grad, sq_sum, sems,
+):
+    slots, item_tiles = live_ref.shape
+    rows = fac.shape[0] // chunks
+    tile = fac.shape[0] // slots
+    width = item.shape[0] // item_tiles
+    per_chunk = slots // chunks
+
+    def rating_copy(i):
+        at = pl.ds(i * rows, rows)
+        return pltpu.make_async_copy(ratings_hbm.at[stratum, at], rating.at[at], sems.at[i])
+
+    for i in range(chunks):
+        rating_copy(i).start()
+    used = (count_ref[0] + per_chunk - 1) // per_chunk
+    sq_sum[...] = jnp.zeros_like(sq_sum)
+    for i in range(chunks):
+        rating_copy(i).wait()
+
+    def one_step(first):
+        half = (item_in if first else item)[...].astype(jnp.bfloat16)
+        item_half[...] = half
+        item_grad[...] = jnp.zeros_like(item_grad)
+
+        def chunk(i, carry):
+            at = pl.ds(pl.multiple_of(i * rows, rows), rows)
+            user = (fac_in if first else fac)[at]
+            user_half = user.astype(jnp.bfloat16)
+            predicted = lax.dot_general(
+                user_half, item_half[...], (((1,), (1,)), ((), ())), preferred_element_type=jnp.float32
+            )
+            squares = None
+            for t in range(per_chunk):
+                for j in range(item_tiles):
+                    block = pl.ds(pl.multiple_of(i * rows + t * tile, tile), tile)
+                    cols = slice(j * width, (j + 1) * width)
+                    diff = predicted[t * tile : (t + 1) * tile, cols] - rating[block, cols].astype(jnp.float32)
+                    masked = diff * live_ref[i * per_chunk + t, j]
+                    err[t * tile : (t + 1) * tile, cols] = masked.astype(jnp.bfloat16)
+                    if first:
+                        part = jnp.sum((masked * diff).reshape(-1, 8, width), axis=0)
+                        squares = part if squares is None else squares + part
+            if first:
+                sq_sum[...] += squares
+            grad = (
+                jnp.dot(err[...], item_half[...], preferred_element_type=jnp.float32) * user_scale
+                + ridge_weight * user
+            )
+            item_grad[...] += grad_of_items(err[...], user_half)
+            new_acc = (acc_in if first else acc)[at] + grad * grad
+            acc[at] = new_acc
+            fac[at] = user - step_rate * grad * lax.rsqrt(new_acc)
+            return carry
+
+        lax.fori_loop(0, used, chunk, 0)
+        old = (item_in if first else item)[...]
+        grad = summed_grad(item_grad[...]) * item_scale + ridge_weight * old
+        new_acc = (item_acc_in if first else item_acc)[...] + grad * grad
+        item_acc[...] = new_acc
+        item[...] = old - step_rate * grad * lax.rsqrt(new_acc)
+
+    for step in range(steps):
+        one_step(step == 0)
+    loss_ref[...] = sq_sum[...]
+
+
+TURNED = True
+
+
+def grad_of_items(err, user_half):
+    pair = (user_half, err) if TURNED else (err, user_half)
+    return lax.dot_general(*pair, (((0,), (0,)), ((), ())), preferred_element_type=jnp.float32)
+
+
+def summed_grad(total):
+    return total.T if TURNED else total
+
+
+def run_stratum(stratum, count, live_tiles, ratings, user_fac, user_acc, item_fac, item_acc):
+    slots = live_tiles.shape[0]
+    user_rows, rank = user_fac.shape
+    item_rows = item_fac.shape[0]
+    chunks = CHUNKS
+    vmem = pl.BlockSpec(memory_space=pltpu.VMEM)
+    smem = pl.BlockSpec(memory_space=pltpu.SMEM)
+    like = [jax.ShapeDtypeStruct(x.shape, x.dtype) for x in (user_fac, user_acc, item_fac, item_acc)]
+    return pl.pallas_call(
+        functools.partial(
+            stratum_kernel, stratum, STEPS, chunks,
+            float(item_rows) ** (-0.5), float(UT * TILE) ** (-0.5),
+        ),
+        out_shape=like + [jax.ShapeDtypeStruct((8, item_rows // live_tiles.shape[1]), jnp.float32)],
+        in_specs=[smem, smem, pl.BlockSpec(memory_space=pl.ANY)] + [vmem] * 4,
+        out_specs=[vmem] * 5,
+        scratch_shapes=[
+            pltpu.VMEM((user_rows, item_rows), jnp.bfloat16),
+            pltpu.VMEM((user_rows // chunks, item_rows), jnp.bfloat16),
+            pltpu.VMEM((item_rows, rank), jnp.bfloat16),
+            pltpu.VMEM((rank, item_rows) if TURNED else (item_rows, rank), jnp.float32),
+            pltpu.VMEM((8, item_rows // live_tiles.shape[1]), jnp.float32),
+            pltpu.SemaphoreType.DMA((chunks,)),
+        ],
+        compiler_params=pltpu.CompilerParams(vmem_limit_bytes=32 * 1024 * 1024),
+    )(count, live_tiles, ratings, user_fac, user_acc, item_fac, item_acc)
+
+
+CHUNKS = 4
 
 
 def segment_plan(group_size, own_tiles):
@@ -119,27 +203,23 @@
     row_valid = jnp.repeat(valid, tile_size)[:, None] > 0.5
     user_fac = jnp.where(row_valid, fetched(users, segments, tile_size, window, pad_rows), 0.0)
     user_acc = jnp.where(row_valid, fetched(user_accum, segments, tile_size, window, pad_rows), 1.0)
-    held_pair = jnp.stack([items, item_accum])
-    loss_list = []
+    item_fac, item_acc = items, item_accum
+    live_all = tile_mask.astype(jnp.float32) * valid[:, None]
+    sq_list = []
     for stratum in range(strata_count):
-        live_tiles = tile_mask[stratum].astype(jnp.float32) * valid[:, None]
-        item_fac = held_pair[0]
-        item_acc = held_pair[1]
-        for inner in range(STEPS):
-            user_fac, user_acc, item_fac, item_acc, sq_error = update(
-                user_fac, user_acc, item_fac, item_acc, ratings[stratum], live_tiles
-            )
-            if inner == 0:
-                observed = jnp.sum(live_tiles) * float(tile_size * tile_size)
-                total_error, total_count = lax.psum((sq_error, observed), ("row", "col"))
-                loss_list.append(total_error / total_count)
-        held_pair = jnp.stack([item_fac, item_acc])
+        user_fac, user_acc, item_fac, item_acc, squares = run_stratum(
+            stratum, own_count[None], live_all[stratum], ratings, user_fac, user_acc, item_fac, item_acc
+        )
+        sq_list.append(jnp.sum(squares))
         if stratum + 1 < strata_count:
-            held_pair = passed_along(held_pair, ("row", "col"), 1)
-    losses = jnp.stack(loss_list)
+            item_fac = passed_along(item_fac, ("row", "col"), 1)
+            item_acc = passed_along(item_acc, ("row", "col"), 1)
+    observed = jnp.sum(live_all, axis=(1, 2)) * float(tile_size * tile_size)
+    total_error, total_count = lax.psum((jnp.stack(sq_list), observed), ("row", "col"))
+    losses = total_error / total_count
     users_new = returned(jnp.where(row_valid, user_fac, 0.0), segments, tile_size, window)
     accum_new = returned(jnp.where(row_valid, user_acc, 0.0), segments, tile_size, window)
-    return (users_new, accum_new, held_pair[0], held_pair[1], losses)
+    return (users_new, accum_new, item_fac, item_acc, losses)
 
 
 def solution(mesh):

time: 248 us -> 236 us (0.952)
  matrix products: 55.6 us -> 0 us
  Pallas kernels: 0 us -> 17.9 us
  local copies, waits for them, and re-layouts: 13.1 us -> 27.8 us
  starting transfers between devices: 48.3 us -> 61.6 us
  between operations: 9.78 us -> 1.76 us
  waiting for transfers between devices: 58.8 us -> 62.9 us
    dot_general x36 -> x0, matrix products: 55.6 us -> none  [the longest x12 19.2 us: update(): lax.dot_general(user_half, item_half, (((1,), (1,)), ((), ())), preferred...]
    pallas_call x0 -> x4, Pallas kernels: none -> 17.9 us  [run_stratum(): pl.pallas_call(functools.partial(stratum_kernel, stratum, STEPS, chunks,...]
    unnamed x48 -> x44, local copies, waits for them, and re-layouts: 2.18 us -> 18.4 us
    ppermute x3 -> x6, starting transfers between devices: 14.7 us -> 27.3 us  [passed_along(): return lax.ppermute(value, axis, pairs)]
    ppermute x8, waiting for transfers between devices: 9.59 us -> 15.2 us  [returned(): part = lax.ppermute(part, 'col', [(m, home) for home, m in pairs])]
    mul x8 -> x0, local copies, waits for them, and re-layouts: 2.74 us -> none  [the longest x4 2.41 us: update(): residue.reshape(live_tiles.shape[0], tile_size, live_tiles.shape[1], tile...]
    another operation x6 -> x1, other arithmetic: 5.17 us -> 2.64 us  [on_device(): jnp.stack(sq_list)]
    ppermute x3 -> x6, waiting for transfers between devices: 31.3 us -> 29.1 us  [passed_along(): return lax.ppermute(value, axis, pairs)]
  transfers between devices with their start and end apart: 19 -> 22, of which waited for: 6 -> 9; matrix products, arithmetic and copies ran while one was open for 9% -> 8% of each run, Pallas kernels for 0% -> 0%
where the time goes in v2:
time: 236 us; the launch traced here: 233 us
  waiting for transfers between devices  62.9 us (27%)
  starting transfers between devices  61.6 us (26%)
  blocking collectives  46.3 us (20%)
  local copies, waits for them, and re-layouts  27.8 us (12%)
  Pallas kernels  17.9 us (8%)
  other arithmetic  15.1 us (6%)
    psum x1, blocking collectives, on_device(): lax.psum((jnp.stack(sq_list), observed), ('row', 'col'))  46.3 us
    ppermute x6, waiting for transfers between devices, passed_along(): return lax.ppermute(value, axis, pairs)  29.1 us
    ppermute x6, starting transfers between devices, passed_along(): return lax.ppermute(value, axis, pairs)  27.3 us
    ppermute x8, starting transfers between devices, fetched(): parts.append(lax.ppermute(part, 'col', pairs) if step else part)  18.9 us
    ppermute x8, waiting for transfers between devices, fetched(): parts.append(lax.ppermute(part, 'col', pairs) if step else part)  18.6 us
    unnamed x44, local copies, waits for them, and re-layouts  18.4 us
    pallas_call x4, Pallas kernels, run_stratum(): pl.pallas_call(functools.partial(stratum_kernel, stratum, STEPS, chunks,...  17.9 us
    ppermute x8, starting transfers between devices, returned(): part = lax.ppermute(part, 'col', [(m, home) for home, m in pairs])  15.4 us
  transfers between devices with their start and end apart: 22, of which 9 were waited for; matrix products, arithmetic and copies ran while one was open for 8% of the time, Pallas kernels for 0%

profile of v2, /device:TPU:0, one launch (start us, length us, event | category | flops | bytes accessed | tf_op | source)
XLA Modules:
  0.0 233.4 jit_solution(16363590570181197186)
XLA Ops:
  0.6 5.1 %collective-permute-start.5 = (f32[1024,128]{1,0:T(8,128)}, f32[1024,128]{1,0:T(8,128)S(1)}, u32[]{:S(2)}, u32[]{:S(2)}) collective-permute-start(f32[1024,128]{1,0:T(8,128)} %param.11), channel_id=1, source_target_pairs={{0,1},{1,2},{2,3},{4,5},{5,6},{6,7},{8,9},{9,10},{10,11},{12,13},{... | collective-permute-start | bytes 1572872 | tf_op jit(solution)/shard_map/ppermute | solution.py:164
  9.2 5.7 %collective-permute-start.4 = (f32[768,128]{1,0:T(8,128)}, f32[768,128]{1,0:T(8,128)S(1)}, u32[]{:S(2)}, u32[]{:S(2)}) collective-permute-start(f32[768,128]{1,0:T(8,128)} %get-tuple-element.60), channel_id=1, source_target_pairs={{0,2},{4,6},{8,10},{12,14},{16,18},{20,22},{24,26},{28,30}} | collective-permute-start | bytes 1179656 | tf_op jit(solution)/shard_map/ppermute | solution.py:164
  18.3 2.9 %collective-permute-start = (f32[768,128]{1,0:T(8,128)}, f32[768,128]{1,0:T(8,128)S(1)}, u32[]{:S(2)}, u32[]{:S(2)}) collective-permute-start(f32[768,128]{1,0:T(8,128)} %get-tuple-element.62), channel_id=1, source_target_pairs={{0,2},{4,6},{8,10},{12,14},{16,18},{20,22},{24,26},{28,30}} | collective-permute-start | bytes 1179656 | tf_op jit(solution)/shard_map/ppermute | solution.py:164
  28.1 17.2 %collective-permute-done = f32[768,128]{1,0:T(8,128)S(1)} collective-permute-done((f32[768,128]{1,0:T(8,128)}, f32[768,128]{1,0:T(8,128)S(1)}, u32[]{:S(2)}, u32[]{:S(2)}) %collective-permute-start) | collective-permute-done | bytes 393248 | tf_op jit(solution)/shard_map/ppermute | solution.py:164
  49.4 3.9 %shard_map.110 = (f32[2048,128]{1,0:T(8,128)S(1)}, f32[2048,128]{1,0:T(8,128)S(1)}, f32[512,128]{1,0:T(8,128)S(1)}, f32[512,128]{1,0:T(8,128)S(1)}, f32[8,128]{1,0:T(8,128)S(1)}) custom-call(s32[1]{0:T(128)} %bitcast.1.count_ref, f32[16,4]{1,0:T(8,128)S(1)} %copy.12.live_ref, bf16[4,2048,512]{2,1,0:T(8,128)(2,1)S(1)} %bitcast.16, ...), custom_call_target="tpu_custom_call" | custom-call | tf_op jit(solution)/shard_map/pallas_call | solution.py:115
  53.3 11.9 %collective-permute-start.8 = (f32[512,128]{1,0:T(8,128)S(1)}, f32[512,128]{1,0:T(8,128)S(1)}, u32[]{:S(2)}, u32[]{:S(2)}) collective-permute-start(f32[512,128]{1,0:T(8,128)S(1)} %get-tuple-element.27), channel_id=1, source_target_pairs={{0,1},{1,2},{2,3},{3,4},{4,5},{5,6},{6,7},{7,8},{8,9},{9,10},{10,1... | collective-permute-start | bytes 786440 | tf_op jit(solution)/shard_map/ppermute | solution.py:22
  65.3 6.6 %collective-permute-done.8.item_in = f32[512,128]{1,0:T(8,128)S(1)} collective-permute-done((f32[512,128]{1,0:T(8,128)S(1)}, f32[512,128]{1,0:T(8,128)S(1)}, u32[]{:S(2)}, u32[]{:S(2)}) %collective-permute-start.8) | collective-permute-done | bytes 262176 | tf_op jit(solution)/shard_map/ppermute | solution.py:22
  71.9 5.5 %collective-permute-done.9.item_acc_in = f32[512,128]{1,0:T(8,128)S(1)} collective-permute-done((f32[512,128]{1,0:T(8,128)S(1)}, f32[512,128]{1,0:T(8,128)S(1)}, u32[]{:S(2)}, u32[]{:S(2)}) %collective-permute-start.9) | collective-permute-done | bytes 262176 | tf_op jit(solution)/shard_map/ppermute | solution.py:22
  78.1 3.4 %copy-done = bf16[4,2048,512]{2,1,0:T(8,128)(2,1)S(1)} copy-done((bf16[4,2048,512]{2,1,0:T(8,128)(2,1)S(1)}, bf16[4,2048,512]{2,1,0:T(8,128)(2,1)}, u32[]{:S(2)}) %copy-start) | copy-done | bytes 8388632
  82.4 4.7 %shard_map.111 = (f32[2048,128]{1,0:T(8,128)S(1)}, f32[2048,128]{1,0:T(8,128)S(1)}, f32[512,128]{1,0:T(8,128)}, f32[512,128]{1,0:T(8,128)}, f32[8,128]{1,0:T(8,128)S(1)}) custom-call(s32[1]{0:T(128)} %bitcast.1.count_ref, f32[16,4]{1,0:T(8,128)S(1)} %copy.13.live_ref, bf16[4,2048,512]{2,1,0:T(8,128)(2,1)S(1)} %copy-done, ...), custom_call_target="tpu_custom_call" | custom-call | tf_op jit(solution)/shard_map/pallas_call | solution.py:115
  88.5 7.2 %collective-permute-start.11 = (f32[512,128]{1,0:T(8,128)}, f32[512,128]{1,0:T(8,128)S(1)}, u32[]{:S(2)}, u32[]{:S(2)}) collective-permute-start(f32[512,128]{1,0:T(8,128)} %get-tuple-element.32), channel_id=1, source_target_pairs={{0,1},{1,2},{2,3},{3,4},{4,5},{5,6},{6,7},{7,8},{8,9},{9,10},{10,1... | collective-permute-start | bytes 786440 | tf_op jit(solution)/shard_map/ppermute | solution.py:22
  95.7 4.2 %collective-permute-done.10.item_in = f32[512,128]{1,0:T(8,128)S(1)} collective-permute-done((f32[512,128]{1,0:T(8,128)}, f32[512,128]{1,0:T(8,128)S(1)}, u32[]{:S(2)}, u32[]{:S(2)}) %collective-permute-start.10) | collective-permute-done | bytes 262176 | tf_op jit(solution)/shard_map/ppermute | solution.py:22
  99.9 5.6 %collective-permute-done.11.item_acc_in = f32[512,128]{1,0:T(8,128)S(1)} collective-permute-done((f32[512,128]{1,0:T(8,128)}, f32[512,128]{1,0:T(8,128)S(1)}, u32[]{:S(2)}, u32[]{:S(2)}) %collective-permute-start.11) | collective-permute-done | bytes 262176 | tf_op jit(solution)/shard_map/ppermute | solution.py:22
  106.2 3.4 %copy-done.1 = bf16[4,2048,512]{2,1,0:T(8,128)(2,1)S(1)} copy-done((bf16[4,2048,512]{2,1,0:T(8,128)(2,1)S(1)}, bf16[4,2048,512]{2,1,0:T(8,128)(2,1)}, u32[]{:S(2)}) %copy-start.1) | copy-done | bytes 8388632
  111.8 4.7 %shard_map.112 = (f32[2048,128]{1,0:T(8,128)S(1)}, f32[2048,128]{1,0:T(8,128)S(1)}, f32[512,128]{1,0:T(8,128)}, f32[512,128]{1,0:T(8,128)}, f32[8,128]{1,0:T(8,128)S(1)}) custom-call(s32[1]{0:T(128)} %bitcast.1.count_ref, f32[16,4]{1,0:T(8,128)S(1)} %copy.14.live_ref, bf16[4,2048,512]{2,1,0:T(8,128)(2,1)S(1)} %copy-done.1, ...), custom_call_target="tpu_custom_call" | custom-call | tf_op jit(solution)/shard_map/pallas_call | solution.py:115
  116.6 7.7 %collective-permute-start.13 = (f32[512,128]{1,0:T(8,128)}, f32[512,128]{1,0:T(8,128)S(1)}, u32[]{:S(2)}, u32[]{:S(2)}) collective-permute-start(f32[512,128]{1,0:T(8,128)} %get-tuple-element.36), channel_id=1, source_target_pairs={{0,1},{1,2},{2,3},{3,4},{4,5},{5,6},{6,7},{7,8},{8,9},{9,10},{10,1... | collective-permute-start | bytes 786440 | tf_op jit(solution)/shard_map/ppermute | solution.py:22
  128.0 5.6 %collective-permute-done.13.item_acc_in = f32[512,128]{1,0:T(8,128)S(1)} collective-permute-done((f32[512,128]{1,0:T(8,128)}, f32[512,128]{1,0:T(8,128)S(1)}, u32[]{:S(2)}, u32[]{:S(2)}) %collective-permute-start.13) | collective-permute-done | bytes 262176 | tf_op jit(solution)/shard_map/ppermute | solution.py:22
  133.6 3.4 %copy-done.2 = bf16[4,2048,512]{2,1,0:T(8,128)(2,1)S(1)} copy-done((bf16[4,2048,512]{2,1,0:T(8,128)(2,1)S(1)}, bf16[4,2048,512]{2,1,0:T(8,128)(2,1)}, u32[]{:S(2)}) %copy-start.2) | copy-done | bytes 8388632
  137.0 4.7 %shard_map.113 = (f32[2048,128]{1,0:T(8,128)S(1)}, f32[2048,128]{1,0:T(8,128)S(1)}, f32[512,128]{1,0:T(8,128)}, f32[512,128]{1,0:T(8,128)}, f32[8,128]{1,0:T(8,128)S(1)}) custom-call(s32[1]{0:T(128)} %bitcast.1.count_ref, f32[16,4]{1,0:T(8,128)S(1)} %copy.15.live_ref, bf16[4,2048,512]{2,1,0:T(8,128)(2,1)S(1)} %copy-done.2, ...), custom_call_target="tpu_custom_call" | custom-call | tf_op jit(solution)/shard_map/pallas_call | solution.py:115
  145.7 5.4 %collective-permute-start.20 = (f32[1024,128]{1,0:T(8,128)}, f32[1024,128]{1,0:T(8,128)}, u32[]{:S(2)}, u32[]{:S(2)}) collective-permute-start(f32[1024,128]{1,0:T(8,128)} %get-tuple-element.54), channel_id=1, source_target_pairs={{0,1},{1,2},{2,3},{4,5},{5,6},{6,7},{8,9},{9,10},{10,11},{12,13},{... | collective-permute-start | bytes 1572872 | tf_op jit(solution)/shard_map/ppermute | solution.py:179
  156.7 15.2 %collective-permute-done.18 = f32[768,128]{1,0:T(8,128)S(1)} collective-permute-done((f32[768,128]{1,0:T(8,128)S(1)}, f32[768,128]{1,0:T(8,128)S(1)}, u32[]{:S(2)}, u32[]{:S(2)}) %collective-permute-start.18) | collective-permute-done | bytes 393248 | tf_op jit(solution)/shard_map/ppermute | solution.py:179
  179.1 2.6 %pad_maximum_fusion = (f32[4]{0:T(128)S(1)}, f32[4]{0:T(128)S(1)}) fusion(f32[1]{0:T(128)} %bitcast.9, f32[1]{0:T(128)} %bitcast.8, f32[1]{0:T(128)} %bitcast.7, f32[1]{0:T(128)} %bitcast.6, f32[4]{0:T(128)S(1)} %get-tuple-element.49), kind=kLoop, calls=%fused_computation.33 | loop fusion | flops 16 | bytes 64 | tf_op jit(solution)/shard_map/stack | solution.py:218
  181.7 46.3 %all-reduce.4 = (f32[4]{0:T(128)S(1)}, f32[4]{0:T(128)S(1)}) all-reduce(f32[4]{0:T(128)S(1)} %get-tuple-element.69, f32[4]{0:T(128)S(1)} %get-tuple-element.70), channel_id=1, replica_groups=mesh['row'=8,'col'=4] {'row','col'}, use_global_device_ids=true, to_apply=%region_6.7 | all-reduce | flops 8 | bytes 64 | tf_op jit(solution)/shard_map/psum | solution.py:218
  228.6 2.5 %fusion.1 = f32[1024,128]{1,0:T(8,128)} fusion(f32[1024,128]{1,0:T(8,128)} %collective-permute-done.20, f32[6656,128]{1,0:T(8,128)} %copy-done.11, f32[768,128]{1,0:T(8,128)} %collective-permute-done.21, f32[1024,128]{1,0:T(8,128)} %collective-permute-done.19, f32[768,128]{1,0:T(8,128)} %copy-done.14), kind=kLoop, calls=%fused_computation.6 | loop fusion | flops 524288 | bytes 2883584 | tf_op jit(solution)/shard_map/add | solution.py:181
  (101 shorter events, 46.4 us)
Async XLA Ops:
  0.6 46.2 %copy-start.12 = (f32[1024,128]{1,0:T(8,128)S(1)}, f32[1024,128]{1,0:T(8,128)}, u32[]{:S(2)}) copy-start(f32[1024,128]{1,0:T(8,128)} %param.11) | copy-start | bytes 1572868
  0.6 45.4 %collective-permute-start.5 = (f32[1024,128]{1,0:T(8,128)}, f32[1024,128]{1,0:T(8,128)S(1)}, u32[]{:S(2)}, u32[]{:S(2)}) collective-permute-start(f32[1024,128]{1,0:T(8,128)} %param.11), channel_id=1, source_target_pairs={{0,1},{1,2},{2,3},{4,5},{5,6},{6,7},{8,9},{9,10},{10,11},{12,13},{... | collective-permute-start | bytes 1572872 | tf_op jit(solution)/shard_map/ppermute | solution.py:164
  5.7 41.2 %collective-permute-start.6 = (f32[1024,128]{1,0:T(8,128)}, f32[1024,128]{1,0:T(8,128)S(1)}, u32[]{:S(2)}, u32[]{:S(2)}) collective-permute-start(f32[1024,128]{1,0:T(8,128)} %param.11), channel_id=1, source_target_pairs={{1,0},{2,1},{3,2},{5,4},{6,5},{7,6},{9,8},{10,9},{11,10},{13,12},{... | collective-permute-start | bytes 1572872 | tf_op jit(solution)/shard_map/ppermute | solution.py:164
  9.2 37.7 %copy-start.13 = (f32[1024,128]{1,0:T(8,128)S(1)}, f32[1024,128]{1,0:T(8,128)}, u32[]{:S(2)}) copy-start(f32[1024,128]{1,0:T(8,128)} %param.10) | copy-start | bytes 1572868
  9.2 17.6 %collective-permute-start.4 = (f32[768,128]{1,0:T(8,128)}, f32[768,128]{1,0:T(8,128)S(1)}, u32[]{:S(2)}, u32[]{:S(2)}) collective-permute-start(f32[768,128]{1,0:T(8,128)} %get-tuple-element.60), channel_id=1, source_target_pairs={{0,2},{4,6},{8,10},{12,14},{16,18},{20,22},{24,26},{28,30}} | collective-permute-start | bytes 1179656 | tf_op jit(solution)/shard_map/ppermute | solution.py:164
  14.8 32.0 %collective-permute-start.1 = (f32[1024,128]{1,0:T(8,128)}, f32[1024,128]{1,0:T(8,128)S(1)}, u32[]{:S(2)}, u32[]{:S(2)}) collective-permute-start(f32[1024,128]{1,0:T(8,128)} %param.10), channel_id=1, source_target_pairs={{0,1},{1,2},{2,3},{4,5},{5,6},{6,7},{8,9},{9,10},{10,11},{12,13},{... | collective-permute-start | bytes 1572872 | tf_op jit(solution)/shard_map/ppermute | solution.py:164
  18.3 27.1 %collective-permute-start = (f32[768,128]{1,0:T(8,128)}, f32[768,128]{1,0:T(8,128)S(1)}, u32[]{:S(2)}, u32[]{:S(2)}) collective-permute-start(f32[768,128]{1,0:T(8,128)} %get-tuple-element.62), channel_id=1, source_target_pairs={{0,2},{4,6},{8,10},{12,14},{16,18},{20,22},{24,26},{28,30}} | collective-permute-start | bytes 1179656 | tf_op jit(solution)/shard_map/ppermute | solution.py:164
  26.8 20.3 %collective-permute-start.2 = (f32[1024,128]{1,0:T(8,128)}, f32[1024,128]{1,0:T(8,128)S(1)}, u32[]{:S(2)}, u32[]{:S(2)}) collective-permute-start(f32[1024,128]{1,0:T(8,128)} %param.10), channel_id=1, source_target_pairs={{1,0},{2,1},{3,2},{5,4},{6,5},{7,6},{9,8},{10,9},{11,10},{13,12},{... | collective-permute-start | bytes 1572872 | tf_op jit(solution)/shard_map/ppermute | solution.py:164
  45.3 1.7 collective-permute-start.7
  46.1 1.2 collective-permute-start.3
  53.3 18.6 %collective-permute-start.8 = (f32[512,128]{1,0:T(8,128)S(1)}, f32[512,128]{1,0:T(8,128)S(1)}, u32[]{:S(2)}, u32[]{:S(2)}) collective-permute-start(f32[512,128]{1,0:T(8,128)S(1)} %get-tuple-element.27), channel_id=1, source_target_pairs={{0,1},{1,2},{2,3},{3,4},{4,5},{5,6},{6,7},{7,8},{8,9},{9,10},{10,1... | collective-permute-start | bytes 786440 | tf_op jit(solution)/shard_map/ppermute | solution.py:22
  65.1 12.3 %collective-permute-start.9 = (f32[512,128]{1,0:T(8,128)S(1)}, f32[512,128]{1,0:T(8,128)S(1)}, u32[]{:S(2)}, u32[]{:S(2)}) collective-permute-start(f32[512,128]{1,0:T(8,128)S(1)} %get-tuple-element.28), channel_id=1, source_target_pairs={{0,1},{1,2},{2,3},{3,4},{4,5},{5,6},{6,7},{7,8},{8,9},{9,10},{10,1... | collective-permute-start | bytes 786440 | tf_op jit(solution)/shard_map/ppermute | solution.py:22
  88.1 11.8 %collective-permute-start.10 = (f32[512,128]{1,0:T(8,128)}, f32[512,128]{1,0:T(8,128)S(1)}, u32[]{:S(2)}, u32[]{:S(2)}) collective-permute-start(f32[512,128]{1,0:T(8,128)} %get-tuple-element.31), channel_id=1, source_target_pairs={{0,1},{1,2},{2,3},{3,4},{4,5},{5,6},{6,7},{7,8},{8,9},{9,10},{10,1... | collective-permute-start | bytes 786440 | tf_op jit(solution)/shard_map/ppermute | solution.py:22
  88.5 17.1 %collective-permute-start.11 = (f32[512,128]{1,0:T(8,128)}, f32[512,128]{1,0:T(8,128)S(1)}, u32[]{:S(2)}, u32[]{:S(2)}) collective-permute-start(f32[512,128]{1,0:T(8,128)} %get-tuple-element.32), channel_id=1, source_target_pairs={{0,1},{1,2},{2,3},{3,4},{4,5},{5,6},{6,7},{7,8},{8,9},{9,10},{10,1... | collective-permute-start | bytes 786440 | tf_op jit(solution)/shard_map/ppermute | solution.py:22
  116.5 11.5 %collective-permute-start.12 = (f32[512,128]{1,0:T(8,128)}, f32[512,128]{1,0:T(8,128)S(1)}, u32[]{:S(2)}, u32[]{:S(2)}) collective-permute-start(f32[512,128]{1,0:T(8,128)} %get-tuple-element.35), channel_id=1, source_target_pairs={{0,1},{1,2},{2,3},{3,4},{4,5},{5,6},{6,7},{7,8},{8,9},{9,10},{10,1... | collective-permute-start | bytes 786440 | tf_op jit(solution)/shard_map/ppermute | solution.py:22
  116.6 17.0 %collective-permute-start.13 = (f32[512,128]{1,0:T(8,128)}, f32[512,128]{1,0:T(8,128)S(1)}, u32[]{:S(2)}, u32[]{:S(2)}) collective-permute-start(f32[512,128]{1,0:T(8,128)} %get-tuple-element.36), channel_id=1, source_target_pairs={{0,1},{1,2},{2,3},{3,4},{4,5},{5,6},{6,7},{7,8},{8,9},{9,10},{10,1... | collective-permute-start | bytes 786440 | tf_op jit(solution)/shard_map/ppermute | solution.py:22
  144.4 33.3 %collective-permute-start.19 = (f32[1024,128]{1,0:T(8,128)}, f32[1024,128]{1,0:T(8,128)}, u32[]{:S(2)}, u32[]{:S(2)}) collective-permute-start(f32[1024,128]{1,0:T(8,128)} %get-tuple-element.53), channel_id=1, source_target_pairs={{1,0},{2,1},{3,2},{5,4},{6,5},{7,6},{9,8},{10,9},{11,10},{13,12},{... | collective-permute-start | bytes 1572872 | tf_op jit(solution)/shard_map/ppermute | solution.py:179
  145.7 82.9 %collective-permute-start.20 = (f32[1024,128]{1,0:T(8,128)}, f32[1024,128]{1,0:T(8,128)}, u32[]{:S(2)}, u32[]{:S(2)}) collective-permute-start(f32[1024,128]{1,0:T(8,128)} %get-tuple-element.54), channel_id=1, source_target_pairs={{0,1},{1,2},{2,3},{4,5},{5,6},{6,7},{8,9},{9,10},{10,11},{12,13},{... | collective-permute-start | bytes 1572872 | tf_op jit(solution)/shard_map/ppermute | solution.py:179
  151.0 20.8 %collective-permute-start.18 = (f32[768,128]{1,0:T(8,128)S(1)}, f32[768,128]{1,0:T(8,128)S(1)}, u32[]{:S(2)}, u32[]{:S(2)}) collective-permute-start(f32[768,128]{1,0:T(8,128)S(1)} %get-tuple-element.51), channel_id=1, source_target_pairs={{2,0},{6,4},{10,8},{14,12},{18,16},{22,20},{26,24},{30,28}} | collective-permute-start | bytes 1179656 | tf_op jit(solution)/shard_map/ppermute | solution.py:179
  152.3 24.1 %collective-permute-start.21 = (f32[768,128]{1,0:T(8,128)}, f32[768,128]{1,0:T(8,128)}, u32[]{:S(2)}, u32[]{:S(2)}) collective-permute-start(f32[768,128]{1,0:T(8,128)} %get-tuple-element.52), channel_id=1, source_target_pairs={{1,3},{5,7},{9,11},{13,15},{17,19},{21,23},{25,27},{29,31}} | collective-permute-start | bytes 1179656 | tf_op jit(solution)/shard_map/ppermute | solution.py:179
  155.4 75.7 %collective-permute-start.15 = (f32[1024,128]{1,0:T(8,128)}, f32[1024,128]{1,0:T(8,128)}, u32[]{:S(2)}, u32[]{:S(2)}) collective-permute-start(f32[1024,128]{1,0:T(8,128)} %get-tuple-element.57), channel_id=1, source_target_pairs={{1,0},{2,1},{3,2},{5,4},{6,5},{7,6},{9,8},{10,9},{11,10},{13,12},{... | collective-permute-start | bytes 1572872 | tf_op jit(solution)/shard_map/ppermute | solution.py:179
  172.7 58.4 %collective-permute-start.16 = (f32[1024,128]{1,0:T(8,128)}, f32[1024,128]{1,0:T(8,128)}, u32[]{:S(2)}, u32[]{:S(2)}) collective-permute-start(f32[1024,128]{1,0:T(8,128)} %get-tuple-element.58), channel_id=1, source_target_pairs={{0,1},{1,2},{2,3},{4,5},{5,6},{6,7},{8,9},{9,10},{10,11},{12,13},{... | collective-permute-start | bytes 1572872 | tf_op jit(solution)/shard_map/ppermute | solution.py:179
  176.4 54.7 %collective-permute-start.14 = (f32[768,128]{1,0:T(8,128)}, f32[768,128]{1,0:T(8,128)}, u32[]{:S(2)}, u32[]{:S(2)}) collective-permute-start(f32[768,128]{1,0:T(8,128)} %get-tuple-element.55), channel_id=1, source_target_pairs={{2,0},{6,4},{10,8},{14,12},{18,16},{22,20},{26,24},{30,28}} | collective-permute-start | bytes 1179656 | tf_op jit(solution)/shard_map/ppermute | solution.py:179
  177.7 53.4 %collective-permute-start.17 = (f32[768,128]{1,0:T(8,128)}, f32[768,128]{1,0:T(8,128)}, u32[]{:S(2)}, u32[]{:S(2)}) collective-permute-start(f32[768,128]{1,0:T(8,128)} %get-tuple-element.56), channel_id=1, source_target_pairs={{1,3},{5,7},{9,11},{13,15},{17,19},{21,23},{25,27},{29,31}} | collective-permute-start | bytes 1179656 | tf_op jit(solution)/shard_map/ppermute | solution.py:179
  (15 other events, 54.4 us)

commit v3 on v2

--- a/solution.py
+++ b/solution.py
@@ -24,10 +24,11 @@
 
 def stratum_kernel(
     stratum, steps, chunks, user_scale, item_scale,
-    count_ref, live_ref, ratings_hbm, fac_in, acc_in, item_in, item_acc_in,
-    fac, acc, item, item_acc, loss_ref,
+    count_ref, live_ref, ratings_hbm, fac_in, acc_in, pair_in,
+    fac, acc, pair, loss_ref,
     rating, err, item_half, item_grad, sq_sum, sems,
 ):
+    item_in, item_acc_in, item, item_acc = pair_in.at[0], pair_in.at[1], pair.at[0], pair.at[1]
     slots, item_tiles = live_ref.shape
     rows = fac.shape[0] // chunks
     tile = fac.shape[0] // slots
@@ -104,22 +105,22 @@
     return total.T if TURNED else total
 
 
-def run_stratum(stratum, count, live_tiles, ratings, user_fac, user_acc, item_fac, item_acc):
+def run_stratum(stratum, count, live_tiles, ratings, user_fac, user_acc, held_pair):
     slots = live_tiles.shape[0]
     user_rows, rank = user_fac.shape
-    item_rows = item_fac.shape[0]
+    item_rows = held_pair.shape[1]
     chunks = CHUNKS
     vmem = pl.BlockSpec(memory_space=pltpu.VMEM)
     smem = pl.BlockSpec(memory_space=pltpu.SMEM)
-    like = [jax.ShapeDtypeStruct(x.shape, x.dtype) for x in (user_fac, user_acc, item_fac, item_acc)]
+    like = [jax.ShapeDtypeStruct(x.shape, x.dtype) for x in (user_fac, user_acc, held_pair)]
     return pl.pallas_call(
         functools.partial(
             stratum_kernel, stratum, STEPS, chunks,
             float(item_rows) ** (-0.5), float(UT * TILE) ** (-0.5),
         ),
         out_shape=like + [jax.ShapeDtypeStruct((8, item_rows // live_tiles.shape[1]), jnp.float32)],
-        in_specs=[smem, smem, pl.BlockSpec(memory_space=pl.ANY)] + [vmem] * 4,
-        out_specs=[vmem] * 5,
+        in_specs=[smem, smem, pl.BlockSpec(memory_space=pl.ANY)] + [vmem] * 3,
+        out_specs=[vmem] * 4,
         scratch_shapes=[
             pltpu.VMEM((user_rows, item_rows), jnp.bfloat16),
             pltpu.VMEM((user_rows // chunks, item_rows), jnp.bfloat16),
@@ -128,8 +129,8 @@
             pltpu.VMEM((8, item_rows // live_tiles.shape[1]), jnp.float32),
             pltpu.SemaphoreType.DMA((chunks,)),
         ],
-        compiler_params=pltpu.CompilerParams(vmem_limit_bytes=32 * 1024 * 1024),
-    )(count, live_tiles, ratings, user_fac, user_acc, item_fac, item_acc)
+        compiler_params=pltpu.CompilerParams(vmem_limit_bytes=52 * 1024 * 1024),
+    )(count, live_tiles, ratings, user_fac, user_acc, held_pair)
 
 
 CHUNKS = 4
@@ -203,23 +204,22 @@
     row_valid = jnp.repeat(valid, tile_size)[:, None] > 0.5
     user_fac = jnp.where(row_valid, fetched(users, segments, tile_size, window, pad_rows), 0.0)
     user_acc = jnp.where(row_valid, fetched(user_accum, segments, tile_size, window, pad_rows), 1.0)
-    item_fac, item_acc = items, item_accum
+    held_pair = jnp.stack([items, item_accum])
     live_all = tile_mask.astype(jnp.float32) * valid[:, None]
     sq_list = []
     for stratum in range(strata_count):
-        user_fac, user_acc, item_fac, item_acc, squares = run_stratum(
-            stratum, own_count[None], live_all[stratum], ratings, user_fac, user_acc, item_fac, item_acc
+        user_fac, user_acc, held_pair, squares = run_stratum(
+            stratum, own_count[None], live_all[stratum], ratings, user_fac, user_acc, held_pair
         )
         sq_list.append(jnp.sum(squares))
         if stratum + 1 < strata_count:
-            item_fac = passed_along(item_fac, ("row", "col"), 1)
-            item_acc = passed_along(item_acc, ("row", "col"), 1)
+            held_pair = passed_along(held_pair, ("row", "col"), 1)
     observed = jnp.sum(live_all, axis=(1, 2)) * float(tile_size * tile_size)
     total_error, total_count = lax.psum((jnp.stack(sq_list), observed), ("row", "col"))
-    losses = total_error / total_count
+    losses, user_fac, user_acc = lax.optimization_barrier((total_error / total_count, user_fac, user_acc))
     users_new = returned(jnp.where(row_valid, user_fac, 0.0), segments, tile_size, window)
     accum_new = returned(jnp.where(row_valid, user_acc, 0.0), segments, tile_size, window)
-    return (users_new, accum_new, item_fac, item_acc, losses)
+    return (users_new, accum_new, held_pair[0], held_pair[1], losses)
 
 
 def solution(mesh):

time: 236 us -> 237 us (level); the launches traced: 233 us -> 238 us
  Pallas kernels: 17.9 us -> 51.9 us
  starting transfers between devices: 61.6 us -> 39.7 us
  waiting for transfers between devices: 62.9 us -> 84.3 us
  local copies, waits for them, and re-layouts: 27.8 us -> 8.82 us
  blocking collectives: 46.3 us -> 36.8 us
    pallas_call x4, Pallas kernels: 17.9 us -> 51.9 us  [run_stratum(): pl.pallas_call(functools.partial(stratum_kernel, stratum, STEPS, chunks,...]
    ppermute x6 -> x3, starting transfers between devices: 27.3 us -> 6.79 us  [passed_along(): return lax.ppermute(value, axis, pairs)]
    unnamed x44 -> x24, local copies, waits for them, and re-layouts: 18.4 us -> 1.36 us
    ppermute x8, waiting for transfers between devices: 15.2 us -> 29.4 us  [returned(): part = lax.ppermute(part, 'col', [(m, home) for home, m in pairs])]
    ppermute x6 -> x3, waiting for transfers between devices: 29.1 us -> 39.8 us  [passed_along(): return lax.ppermute(value, axis, pairs)]
    psum x1, blocking collectives: 46.3 us -> 36.8 us  [on_device(): lax.psum((jnp.stack(sq_list), observed), ('row', 'col'))]
    slice x4, local copies, waits for them, and re-layouts: 4.19 us -> 0.25 us  [returned(): part = frame[at:at + length]]
    ppermute x8, waiting for transfers between devices: 18.6 us -> 15.1 us  [fetched(): parts.append(lax.ppermute(part, 'col', pairs) if step else part)]
  transfers between devices with their start and end apart: 22 -> 19, of which waited for: 9 -> 6; matrix products, arithmetic and copies ran while one was open for 8% -> 7% of each run, Pallas kernels for 0% -> 0%
where the time goes in v3:
time: 237 us; the launch traced here: 238 us
  waiting for transfers between devices  84.3 us (36%)
  Pallas kernels  51.9 us (22%)
  starting transfers between devices  39.7 us (17%)
  blocking collectives  36.8 us (16%)
  other arithmetic  14.9 us (6%)
  local copies, waits for them, and re-layouts  8.82 us (4%)
    pallas_call x4, Pallas kernels, run_stratum(): pl.pallas_call(functools.partial(stratum_kernel, stratum, STEPS, chunks,...  51.9 us
    ppermute x3, waiting for transfers between devices, passed_along(): return lax.ppermute(value, axis, pairs)  39.8 us
    psum x1, blocking collectives, on_device(): lax.psum((jnp.stack(sq_list), observed), ('row', 'col'))  36.8 us
    ppermute x8, waiting for transfers between devices, returned(): part = lax.ppermute(part, 'col', [(m, home) for home, m in pairs])  29.4 us
    ppermute x8, starting transfers between devices, fetched(): parts.append(lax.ppermute(part, 'col', pairs) if step else part)  19.5 us
    ppermute x8, waiting for transfers between devices, fetched(): parts.append(lax.ppermute(part, 'col', pairs) if step else part)  15.1 us
    ppermute x8, starting transfers between devices, returned(): part = lax.ppermute(part, 'col', [(m, home) for home, m in pairs])  13.4 us
    ppermute x3, starting transfers between devices, passed_along(): return lax.ppermute(value, axis, pairs)  6.79 us
  transfers between devices with their start and end apart: 19, of which 6 were waited for; matrix products, arithmetic and copies ran while one was open for 7% of the time, Pallas kernels for 0%

profile of v3, /device:TPU:0, one launch (start us, length us, event | category | flops | bytes accessed | tf_op | source)
XLA Modules:
  0.0 238.2 jit_solution(14664009394907157941)
XLA Ops:
  0.7 5.1 %collective-permute-start.5 = (f32[1024,128]{1,0:T(8,128)}, f32[1024,128]{1,0:T(8,128)S(1)}, u32[]{:S(2)}, u32[]{:S(2)}) collective-permute-start(f32[1024,128]{1,0:T(8,128)} %param.11), channel_id=1, source_target_pairs={{0,1},{1,2},{2,3},{4,5},{5,6},{6,7},{8,9},{9,10},{10,11},{12,13},{... | collective-permute-start | bytes 1572872 | tf_op jit(solution)/shard_map/ppermute | solution.py:165
  7.1 2.0 fusion.11
  9.1 5.5 %collective-permute-start.4 = (f32[768,128]{1,0:T(8,128)}, f32[768,128]{1,0:T(8,128)S(1)}, u32[]{:S(2)}, u32[]{:S(2)}) collective-permute-start(f32[768,128]{1,0:T(8,128)} %get-tuple-element.60), channel_id=1, source_target_pairs={{0,2},{4,6},{8,10},{12,14},{16,18},{20,22},{24,26},{28,30}} | collective-permute-start | bytes 1179656 | tf_op jit(solution)/shard_map/ppermute | solution.py:165
  14.6 1.3 collective-permute-start.1
  16.0 2.1 fusion.12
  18.1 3.6 %collective-permute-start = (f32[768,128]{1,0:T(8,128)}, f32[768,128]{1,0:T(8,128)}, u32[]{:S(2)}, u32[]{:S(2)}) collective-permute-start(f32[768,128]{1,0:T(8,128)} %get-tuple-element.62), channel_id=1, source_target_pairs={{0,2},{4,6},{8,10},{12,14},{16,18},{20,22},{24,26},{28,30}} | collective-permute-start | bytes 1179656 | tf_op jit(solution)/shard_map/ppermute | solution.py:165
  21.7 1.4 fusion.4
  23.8 1.4 fusion.6
  30.3 15.1 %collective-permute-done = f32[768,128]{1,0:T(8,128)} collective-permute-done((f32[768,128]{1,0:T(8,128)}, f32[768,128]{1,0:T(8,128)}, u32[]{:S(2)}, u32[]{:S(2)}) %collective-permute-start) | collective-permute-done | bytes 393248 | tf_op jit(solution)/shard_map/ppermute | solution.py:165
  48.3 1.7 dynamic-slice_select_fusion
  50.0 13.0 %shard_map.110 = (f32[2048,128]{1,0:T(8,128)}, f32[2048,128]{1,0:T(8,128)}, f32[2,512,128]{2,1,0:T(8,128)S(1)}, f32[8,128]{1,0:T(8,128)S(1)}) custom-call(s32[1]{0:T(128)} %bitcast.1.count_ref, f32[16,4]{1,0:T(8,128)S(1)} %copy.12.live_ref, bf16[4,2048,512]{2,1,0:T(8,128)(2,1)} %ratings_hbm.7, f32[2048,128]{1,0:T(8,128)} %get-tuple-element.68.fac_in, ...), custom_call_target="tpu_custom_call" | custom-call | tf_op jit(solution)/shard_map/pallas_call | solution.py:116
  63.0 6.7 %collective-permute-start.8 = (f32[2,512,128]{2,1,0:T(8,128)S(1)}, f32[2,512,128]{2,1,0:T(8,128)S(1)}, u32[]{:S(2)}, u32[]{:S(2)}) collective-permute-start(f32[2,512,128]{2,1,0:T(8,128)S(1)} %get-tuple-element.27), channel_id=1, source_target_pairs={{0,1},{1,2},{2,3},{3,4},{4,5},{5,6},{6,7},{7,8},{8,9},{9,10},{10,1... | collective-permute-start | bytes 1572872 | tf_op jit(solution)/shard_map/ppermute | solution.py:22
  69.7 11.7 %collective-permute-done.8.pair_in = f32[2,512,128]{2,1,0:T(8,128)S(1)} collective-permute-done((f32[2,512,128]{2,1,0:T(8,128)S(1)}, f32[2,512,128]{2,1,0:T(8,128)S(1)}, u32[]{:S(2)}, u32[]{:S(2)}) %collective-permute-start.8) | collective-permute-done | bytes 524320 | tf_op jit(solution)/shard_map/ppermute | solution.py:22
  81.4 13.0 %shard_map.111 = (f32[2048,128]{1,0:T(8,128)}, f32[2048,128]{1,0:T(8,128)}, f32[2,512,128]{2,1,0:T(8,128)S(1)}, f32[8,128]{1,0:T(8,128)S(1)}) custom-call(s32[1]{0:T(128)} %bitcast.1.count_ref, f32[16,4]{1,0:T(8,128)S(1)} %copy.13.live_ref, bf16[4,2048,512]{2,1,0:T(8,128)(2,1)} %ratings_hbm.7, f32[2048,128]{1,0:T(8,128)} %get-tuple-element.25.fac_in, ...), custom_call_target="tpu_custom_call" | custom-call | tf_op jit(solution)/shard_map/pallas_call | solution.py:116
  94.5 17.2 %collective-permute-done.9.pair_in = f32[2,512,128]{2,1,0:T(8,128)S(1)} collective-permute-done((f32[2,512,128]{2,1,0:T(8,128)S(1)}, f32[2,512,128]{2,1,0:T(8,128)S(1)}, u32[]{:S(2)}, u32[]{:S(2)}) %collective-permute-start.9) | collective-permute-done | bytes 524320 | tf_op jit(solution)/shard_map/ppermute | solution.py:22
  111.8 13.0 %shard_map.112 = (f32[2048,128]{1,0:T(8,128)}, f32[2048,128]{1,0:T(8,128)}, f32[2,512,128]{2,1,0:T(8,128)S(1)}, f32[8,128]{1,0:T(8,128)S(1)}) custom-call(s32[1]{0:T(128)} %bitcast.1.count_ref, f32[16,4]{1,0:T(8,128)S(1)} %copy.14.live_ref, bf16[4,2048,512]{2,1,0:T(8,128)(2,1)} %ratings_hbm.7, f32[2048,128]{1,0:T(8,128)} %get-tuple-element.29.fac_in, ...), custom_call_target="tpu_custom_call" | custom-call | tf_op jit(solution)/shard_map/pallas_call | solution.py:116
  126.7 10.9 %collective-permute-done.10.pair_in = f32[2,512,128]{2,1,0:T(8,128)S(1)} collective-permute-done((f32[2,512,128]{2,1,0:T(8,128)S(1)}, f32[2,512,128]{2,1,0:T(8,128)S(1)}, u32[]{:S(2)}, u32[]{:S(2)}) %collective-permute-start.10) | collective-permute-done | bytes 524320 | tf_op jit(solution)/shard_map/ppermute | solution.py:22
  137.6 13.0 %shard_map.113 = (f32[2048,128]{1,0:T(8,128)}, f32[2048,128]{1,0:T(8,128)}, f32[2,512,128]{2,1,0:T(8,128)S(1)}, f32[8,128]{1,0:T(8,128)S(1)}) custom-call(s32[1]{0:T(128)} %bitcast.1.count_ref, f32[16,4]{1,0:T(8,128)S(1)} %copy.15.live_ref, bf16[4,2048,512]{2,1,0:T(8,128)(2,1)} %ratings_hbm.7, f32[2048,128]{1,0:T(8,128)} %get-tuple-element.33.fac_in, ...), custom_call_target="tpu_custom_call" | custom-call | tf_op jit(solution)/shard_map/pallas_call | solution.py:116
  151.2 2.7 %pad_maximum_fusion.1 = (f32[4]{0:T(128)S(1)}, f32[4]{0:T(128)S(1)}) fusion(f32[1]{0:T(128)} %bitcast.11, f32[1]{0:T(128)} %bitcast.9, f32[1]{0:T(128)} %bitcast.7, f32[1]{0:T(128)} %bitcast.5, f32[4]{0:T(128)S(1)} %copy-done.6), kind=kLoop, calls=%fused_computation.36 | loop fusion | flops 16 | bytes 64 | tf_op jit(solution)/shard_map/stack | solution.py:218
  153.9 36.8 %all-reduce.4 = (f32[4]{0:T(128)S(1)}, f32[4]{0:T(128)S(1)}) all-reduce(f32[4]{0:T(128)S(1)} %get-tuple-element.69, f32[4]{0:T(128)S(1)} %get-tuple-element.70), channel_id=1, replica_groups=mesh['row'=8,'col'=4] {'row','col'}, use_global_device_ids=true, to_apply=%region_6.7 | all-reduce | flops 8 | bytes 64 | tf_op jit(solution)/shard_map/psum | solution.py:218
  192.0 1.4 collective-permute-start.16
  193.4 5.4 %collective-permute-start.17 = (f32[1024,128]{1,0:T(8,128)S(1)}, f32[1024,128]{1,0:T(8,128)S(1)}, u32[]{:S(2)}, u32[]{:S(2)}) collective-permute-start(f32[1024,128]{1,0:T(8,128)S(1)} %get-tuple-element.52), channel_id=1, source_target_pairs={{0,1},{1,2},{2,3},{4,5},{5,6},{6,7},{8,9},{9,10},{10,11},{12,13},{... | collective-permute-start | bytes 1572872 | tf_op jit(solution)/shard_map/ppermute | solution.py:180
  202.8 16.8 %collective-permute-done.15 = f32[768,128]{1,0:T(8,128)S(1)} collective-permute-done((f32[768,128]{1,0:T(8,128)S(1)}, f32[768,128]{1,0:T(8,128)S(1)}, u32[]{:S(2)}, u32[]{:S(2)}) %collective-permute-start.15) | collective-permute-done | bytes 393248 | tf_op jit(solution)/shard_map/ppermute | solution.py:180
  224.8 12.5 %collective-permute-done.11 = f32[768,128]{1,0:T(8,128)S(1)} collective-permute-done((f32[768,128]{1,0:T(8,128)S(1)}, f32[768,128]{1,0:T(8,128)S(1)}, u32[]{:S(2)}, u32[]{:S(2)}) %collective-permute-start.11) | collective-permute-done | bytes 393248 | tf_op jit(solution)/shard_map/ppermute | solution.py:180
  (76 shorter events, 23.1 us)
Async XLA Ops:
  0.6 47.2 %copy-start = (f32[1024,128]{1,0:T(8,128)S(1)}, f32[1024,128]{1,0:T(8,128)}, u32[]{:S(2)}) copy-start(f32[1024,128]{1,0:T(8,128)} %param.11) | copy-start | bytes 1572868
  0.6 28.3 %copy-start.1 = (f32[1024,128]{1,0:T(8,128)S(1)}, f32[1024,128]{1,0:T(8,128)}, u32[]{:S(2)}) copy-start(f32[1024,128]{1,0:T(8,128)} %param.10) | copy-start | bytes 1572868
  0.7 46.4 %collective-permute-start.5 = (f32[1024,128]{1,0:T(8,128)}, f32[1024,128]{1,0:T(8,128)S(1)}, u32[]{:S(2)}, u32[]{:S(2)}) collective-permute-start(f32[1024,128]{1,0:T(8,128)} %param.11), channel_id=1, source_target_pairs={{0,1},{1,2},{2,3},{4,5},{5,6},{6,7},{8,9},{9,10},{10,11},{12,13},{... | collective-permute-start | bytes 1572872 | tf_op jit(solution)/shard_map/ppermute | solution.py:165
  5.8 42.2 %collective-permute-start.6 = (f32[1024,128]{1,0:T(8,128)}, f32[1024,128]{1,0:T(8,128)S(1)}, u32[]{:S(2)}, u32[]{:S(2)}) collective-permute-start(f32[1024,128]{1,0:T(8,128)} %param.11), channel_id=1, source_target_pairs={{1,0},{2,1},{3,2},{5,4},{6,5},{7,6},{9,8},{10,9},{11,10},{13,12},{... | collective-permute-start | bytes 1572872 | tf_op jit(solution)/shard_map/ppermute | solution.py:165
  9.1 19.8 %collective-permute-start.4 = (f32[768,128]{1,0:T(8,128)}, f32[768,128]{1,0:T(8,128)S(1)}, u32[]{:S(2)}, u32[]{:S(2)}) collective-permute-start(f32[768,128]{1,0:T(8,128)} %get-tuple-element.60), channel_id=1, source_target_pairs={{0,2},{4,6},{8,10},{12,14},{16,18},{20,22},{24,26},{28,30}} | collective-permute-start | bytes 1179656 | tf_op jit(solution)/shard_map/ppermute | solution.py:165
  14.6 33.2 %collective-permute-start.1 = (f32[1024,128]{1,0:T(8,128)}, f32[1024,128]{1,0:T(8,128)S(1)}, u32[]{:S(2)}, u32[]{:S(2)}) collective-permute-start(f32[1024,128]{1,0:T(8,128)} %param.10), channel_id=1, source_target_pairs={{0,1},{1,2},{2,3},{4,5},{5,6},{6,7},{8,9},{9,10},{10,11},{12,13},{... | collective-permute-start | bytes 1572872 | tf_op jit(solution)/shard_map/ppermute | solution.py:165
  18.1 27.3 %collective-permute-start = (f32[768,128]{1,0:T(8,128)}, f32[768,128]{1,0:T(8,128)}, u32[]{:S(2)}, u32[]{:S(2)}) collective-permute-start(f32[768,128]{1,0:T(8,128)} %get-tuple-element.62), channel_id=1, source_target_pairs={{0,2},{4,6},{8,10},{12,14},{16,18},{20,22},{24,26},{28,30}} | collective-permute-start | bytes 1179656 | tf_op jit(solution)/shard_map/ppermute | solution.py:165
  28.9 19.1 %collective-permute-start.2 = (f32[1024,128]{1,0:T(8,128)S(1)}, f32[1024,128]{1,0:T(8,128)S(1)}, u32[]{:S(2)}, u32[]{:S(2)}) collective-permute-start(f32[1024,128]{1,0:T(8,128)S(1)} %copy-done.1), channel_id=1, source_target_pairs={{1,0},{2,1},{3,2},{5,4},{6,5},{7,6},{9,8},{10,9},{11,10},{13,12},{... | collective-permute-start | bytes 1572872 | tf_op jit(solution)/shard_map/ppermute | solution.py:165
  45.3 2.7 %collective-permute-start.7 = (f32[768,128]{1,0:T(8,128)}, f32[768,128]{1,0:T(8,128)S(1)}, u32[]{:S(2)}, u32[]{:S(2)}) collective-permute-start(f32[768,128]{1,0:T(8,128)} %get-tuple-element.59), channel_id=1, source_target_pairs={{3,1},{7,5},{11,9},{15,13},{19,17},{23,21},{27,25},{31,29}} | collective-permute-start | bytes 1179656 | tf_op jit(solution)/shard_map/ppermute | solution.py:165
  47.1 1.1 collective-permute-start.3
  50.0 19.7 %copy-start.5 = (f32[16,4]{0,1:T(4,128)S(1)}, f32[16,4]{0,1:T(4,128)}, u32[]{:S(2)}) copy-start(f32[16,4]{0,1:T(4,128)} %get-tuple-element.66) | copy-start | bytes 772
  63.0 18.4 %collective-permute-start.8 = (f32[2,512,128]{2,1,0:T(8,128)S(1)}, f32[2,512,128]{2,1,0:T(8,128)S(1)}, u32[]{:S(2)}, u32[]{:S(2)}) collective-permute-start(f32[2,512,128]{2,1,0:T(8,128)S(1)} %get-tuple-element.27), channel_id=1, source_target_pairs={{0,1},{1,2},{2,3},{3,4},{4,5},{5,6},{6,7},{7,8},{8,9},{9,10},{10,1... | collective-permute-start | bytes 1572872 | tf_op jit(solution)/shard_map/ppermute | solution.py:22
  94.4 17.4 %collective-permute-start.9 = (f32[2,512,128]{2,1,0:T(8,128)S(1)}, f32[2,512,128]{2,1,0:T(8,128)S(1)}, u32[]{:S(2)}, u32[]{:S(2)}) collective-permute-start(f32[2,512,128]{2,1,0:T(8,128)S(1)} %get-tuple-element.31), channel_id=1, source_target_pairs={{0,1},{1,2},{2,3},{3,4},{4,5},{5,6},{6,7},{7,8},{8,9},{9,10},{10,1... | collective-permute-start | bytes 1572872 | tf_op jit(solution)/shard_map/ppermute | solution.py:22
  124.8 12.9 %collective-permute-start.10 = (f32[2,512,128]{2,1,0:T(8,128)S(1)}, f32[2,512,128]{2,1,0:T(8,128)S(1)}, u32[]{:S(2)}, u32[]{:S(2)}) collective-permute-start(f32[2,512,128]{2,1,0:T(8,128)S(1)} %get-tuple-element.35), channel_id=1, source_target_pairs={{0,1},{1,2},{2,3},{3,4},{4,5},{5,6},{6,7},{7,8},{8,9},{9,10},{10,1... | collective-permute-start | bytes 1572872 | tf_op jit(solution)/shard_map/ppermute | solution.py:22
  137.6 13.6 %copy-start.6 = (f32[4]{0:T(128)S(1)}, f32[4]{0:T(128)}, u32[]{:S(2)}) copy-start(f32[4]{0:T(128)} %get-tuple-element.47) | copy-start | bytes 52
  150.6 40.9 %copy-start.3 = (f32[2048,128]{1,0:T(8,128)S(1)}, f32[2048,128]{1,0:T(8,128)}, u32[]{:S(2)}) copy-start(f32[2048,128]{1,0:T(8,128)} %get-tuple-element.40) | copy-start | bytes 3145732
  192.0 30.4 %collective-permute-start.16 = (f32[1024,128]{1,0:T(8,128)S(1)}, f32[1024,128]{1,0:T(8,128)S(1)}, u32[]{:S(2)}, u32[]{:S(2)}) collective-permute-start(f32[1024,128]{1,0:T(8,128)S(1)} %get-tuple-element.51), channel_id=1, source_target_pairs={{1,0},{2,1},{3,2},{5,4},{6,5},{7,6},{9,8},{10,9},{11,10},{13,12},{... | collective-permute-start | bytes 1572872 | tf_op jit(solution)/shard_map/ppermute | solution.py:180
  193.4 30.5 %collective-permute-start.17 = (f32[1024,128]{1,0:T(8,128)S(1)}, f32[1024,128]{1,0:T(8,128)S(1)}, u32[]{:S(2)}, u32[]{:S(2)}) collective-permute-start(f32[1024,128]{1,0:T(8,128)S(1)} %get-tuple-element.52), channel_id=1, source_target_pairs={{0,1},{1,2},{2,3},{4,5},{5,6},{6,7},{8,9},{9,10},{10,11},{12,13},{... | collective-permute-start | bytes 1572872 | tf_op jit(solution)/shard_map/ppermute | solution.py:180
  198.8 20.8 %collective-permute-start.15 = (f32[768,128]{1,0:T(8,128)S(1)}, f32[768,128]{1,0:T(8,128)S(1)}, u32[]{:S(2)}, u32[]{:S(2)}) collective-permute-start(f32[768,128]{1,0:T(8,128)S(1)} %get-tuple-element.49), channel_id=1, source_target_pairs={{2,0},{6,4},{10,8},{14,12},{18,16},{22,20},{26,24},{30,28}} | collective-permute-start | bytes 1179656 | tf_op jit(solution)/shard_map/ppermute | solution.py:180
  200.1 20.9 %collective-permute-start.18 = (f32[768,128]{1,0:T(8,128)S(1)}, f32[768,128]{1,0:T(8,128)S(1)}, u32[]{:S(2)}, u32[]{:S(2)}) collective-permute-start(f32[768,128]{1,0:T(8,128)S(1)} %get-tuple-element.50), channel_id=1, source_target_pairs={{1,3},{5,7},{9,11},{13,15},{17,19},{21,23},{25,27},{29,31}} | collective-permute-start | bytes 1179656 | tf_op jit(solution)/shard_map/ppermute | solution.py:180
  201.5 35.8 %collective-permute-start.12 = (f32[1024,128]{1,0:T(8,128)S(1)}, f32[1024,128]{1,0:T(8,128)S(1)}, u32[]{:S(2)}, u32[]{:S(2)}) collective-permute-start(f32[1024,128]{1,0:T(8,128)S(1)} %get-tuple-element.55), channel_id=1, source_target_pairs={{1,0},{2,1},{3,2},{5,4},{6,5},{7,6},{9,8},{10,9},{11,10},{13,12},{... | collective-permute-start | bytes 1572872 | tf_op jit(solution)/shard_map/ppermute | solution.py:180
  219.6 17.7 %collective-permute-start.13 = (f32[1024,128]{1,0:T(8,128)S(1)}, f32[1024,128]{1,0:T(8,128)S(1)}, u32[]{:S(2)}, u32[]{:S(2)}) collective-permute-start(f32[1024,128]{1,0:T(8,128)S(1)} %get-tuple-element.56), channel_id=1, source_target_pairs={{0,1},{1,2},{2,3},{4,5},{5,6},{6,7},{8,9},{9,10},{10,11},{12,13},{... | collective-permute-start | bytes 1572872 | tf_op jit(solution)/shard_map/ppermute | solution.py:180
  221.0 16.3 %collective-permute-start.11 = (f32[768,128]{1,0:T(8,128)S(1)}, f32[768,128]{1,0:T(8,128)S(1)}, u32[]{:S(2)}, u32[]{:S(2)}) collective-permute-start(f32[768,128]{1,0:T(8,128)S(1)} %get-tuple-element.53), channel_id=1, source_target_pairs={{2,0},{6,4},{10,8},{14,12},{18,16},{22,20},{26,24},{30,28}} | collective-permute-start | bytes 1179656 | tf_op jit(solution)/shard_map/ppermute | solution.py:180
  222.3 15.0 %collective-permute-start.14 = (f32[768,128]{1,0:T(8,128)S(1)}, f32[768,128]{1,0:T(8,128)S(1)}, u32[]{:S(2)}, u32[]{:S(2)}) collective-permute-start(f32[768,128]{1,0:T(8,128)S(1)} %get-tuple-element.54), channel_id=1, source_target_pairs={{1,3},{5,7},{9,11},{13,15},{17,19},{21,23},{25,27},{29,31}} | collective-permute-start | bytes 1179656 | tf_op jit(solution)/shard_map/ppermute | solution.py:180
  (2 other events, 22.3 us)

commit v4 on v3

--- a/solution.py
+++ b/solution.py
@@ -134,6 +134,62 @@
 
 
 CHUNKS = 4
+
+
+def sum_kernel(axes, x_ref, out_ref, *scratch):
+    barrier = pltpu.get_barrier_semaphore()
+    peers = 0
+    for axis, count in axes:
+        me = lax.axis_index(axis)
+        for k in range(1, count):
+            pl.semaphore_signal(
+                barrier, inc=1, device_id={axis: lax.rem(me + k, count)}, device_id_type=pl.DeviceIdType.MESH
+            )
+        peers += count - 1
+    pl.semaphore_wait(barrier, peers)
+    value = x_ref[...]
+    for (axis, count), at in zip(axes, range(0, len(scratch), 3)):
+        slots, send_sems, recv_sems = scratch[at : at + 3]
+        me = lax.axis_index(axis)
+        slots[0] = value
+        copies = []
+        for k in range(1, count):
+            copy = pltpu.make_async_remote_copy(
+                src_ref=slots.at[0],
+                dst_ref=slots.at[k],
+                send_sem=send_sems.at[k],
+                recv_sem=recv_sems.at[k],
+                device_id={axis: lax.rem(me + k, count)},
+                device_id_type=pl.DeviceIdType.MESH,
+            )
+            copy.start()
+            copies.append(copy)
+        for copy in copies:
+            copy.wait()
+        value = slots[me]
+        for source in range(1, count):
+            value = value + slots[lax.rem(me - source + count, count)]
+    out_ref[...] = value
+
+
+def summed_everywhere(sums):
+    axes = [(axis, lax.axis_size(axis)) for axis in ("col", "row")]
+    scratch = []
+    for axis, count in axes:
+        scratch += [
+            pltpu.VMEM((count,) + sums.shape, sums.dtype),
+            pltpu.SemaphoreType.DMA((count,)),
+            pltpu.SemaphoreType.DMA((count,)),
+        ]
+    vmem = pl.BlockSpec(memory_space=pltpu.VMEM)
+    return pl.pallas_call(
+        functools.partial(sum_kernel, axes),
+        out_shape=jax.ShapeDtypeStruct(sums.shape, sums.dtype),
+        in_specs=[vmem],
+        out_specs=vmem,
+        scratch_shapes=scratch,
+        compiler_params=pltpu.CompilerParams(collective_id=0, has_side_effects=True),
+    )(sums)
 
 
 def segment_plan(group_size, own_tiles):
@@ -215,7 +271,10 @@
         if stratum + 1 < strata_count:
             held_pair = passed_along(held_pair, ("row", "col"), 1)
     observed = jnp.sum(live_all, axis=(1, 2)) * float(tile_size * tile_size)
-    total_error, total_count = lax.psum((jnp.stack(sq_list), observed), ("row", "col"))
+    sums = jnp.concatenate([jnp.stack(sq_list), observed])
+    sums = jnp.broadcast_to(jnp.pad(sums, (0, items.shape[1] - sums.shape[0]))[None, :], (8, items.shape[1]))
+    totals = summed_everywhere(sums)[0]
+    total_error, total_count = totals[:strata_count], totals[strata_count : 2 * strata_count]
     losses, user_fac, user_acc = lax.optimization_barrier((total_error / total_count, user_fac, user_acc))
     users_new = returned(jnp.where(row_valid, user_fac, 0.0), segments, tile_size, window)
     accum_new = returned(jnp.where(row_valid, user_acc, 0.0), segments, tile_size, window)

time: 237 us -> 210 us (0.89); the launches traced: 238 us -> 207 us
  blocking collectives: 36.8 us -> 0 us
  starting transfers between devices: 39.7 us -> 63.8 us
  waiting for transfers between devices: 84.3 us -> 74.2 us
  Pallas kernels: 51.9 us -> 42.1 us
  local copies, waits for them, and re-layouts: 8.82 us -> 12.1 us
    psum x1 -> x0, blocking collectives: 36.8 us -> none  [on_device(): lax.psum((jnp.stack(sq_list), observed), ('row', 'col'))]
    ppermute x3, starting transfers between devices: 6.79 us -> 31.7 us  [passed_along(): return lax.ppermute(value, axis, pairs)]
    pallas_call x4, Pallas kernels: 51.9 us -> 29.2 us  [run_stratum(): pl.pallas_call(functools.partial(stratum_kernel, stratum, STEPS, chunks,...]
    pallas_call x0 -> x1, Pallas kernels: none -> 12.9 us  [summed_everywhere(): pl.pallas_call(functools.partial(sum_kernel, axes), out_shape=jax.ShapeDt...]
    ppermute x3, waiting for transfers between devices: 39.8 us -> 29.9 us  [passed_along(): return lax.ppermute(value, axis, pairs)]
    concatenate x0 -> x1, local copies, waits for them, and re-layouts: none -> 2.67 us  [on_device(): sums = jnp.concatenate([jnp.stack(sq_list), observed])]
    another operation x1 -> x0, other arithmetic: 2.66 us -> none  [on_device(): jnp.stack(sq_list)]
  transfers between devices with their start and end apart: 19 -> 19, of which waited for: 6 -> 6; matrix products, arithmetic and copies ran while one was open for 7% -> 8% of each run, Pallas kernels for 0% -> 0%
where the time goes in v4:
time: 210 us; the launch traced here: 207 us
  waiting for transfers between devices  74.2 us (35%)
  starting transfers between devices  63.8 us (30%)
  Pallas kernels  42.1 us (20%)
  other arithmetic  13 us (6%)
  local copies, waits for them, and re-layouts  12.1 us (6%)
    ppermute x3, starting transfers between devices, passed_along(): return lax.ppermute(value, axis, pairs)  31.7 us
    ppermute x3, waiting for transfers between devices, passed_along(): return lax.ppermute(value, axis, pairs)  29.9 us
    pallas_call x4, Pallas kernels, run_stratum(): pl.pallas_call(functools.partial(stratum_kernel, stratum, STEPS, chunks,...  29.2 us
    ppermute x8, waiting for transfers between devices, returned(): part = lax.ppermute(part, 'col', [(m, home) for home, m in pairs])  29.1 us
    ppermute x8, starting transfers between devices, fetched(): parts.append(lax.ppermute(part, 'col', pairs) if step else part)  19.5 us
    ppermute x8, waiting for transfers between devices, fetched(): parts.append(lax.ppermute(part, 'col', pairs) if step else part)  15.2 us
    pallas_call x1, Pallas kernels, summed_everywhere(): pl.pallas_call(functools.partial(sum_kernel, axes), out_shape=jax.ShapeDt...  12.9 us
    ppermute x8, starting transfers between devices, returned(): part = lax.ppermute(part, 'col', [(m, home) for home, m in pairs])  12.6 us
  transfers between devices with their start and end apart: 19, of which 6 were waited for; matrix products, arithmetic and copies ran while one was open for 8% of the time, Pallas kernels for 0%

profile of v4, /device:TPU:0, one launch (start us, length us, event | category | flops | bytes accessed | tf_op | source)
XLA Modules:
  0.0 206.9 jit_solution(9909416968566895092)
XLA Ops:
  0.7 5.1 %collective-permute-start.5 = (f32[1024,128]{1,0:T(8,128)}, f32[1024,128]{1,0:T(8,128)S(1)}, u32[]{:S(2)}, u32[]{:S(2)}) collective-permute-start(f32[1024,128]{1,0:T(8,128)} %param.11), channel_id=1, source_target_pairs={{0,1},{1,2},{2,3},{4,5},{5,6},{6,7},{8,9},{9,10},{10,11},{12,13},{... | collective-permute-start | bytes 1572872 | tf_op jit(solution)/shard_map/ppermute | solution.py:221
  7.1 2.0 fusion.12
  9.1 5.5 %collective-permute-start.4 = (f32[768,128]{1,0:T(8,128)}, f32[768,128]{1,0:T(8,128)S(1)}, u32[]{:S(2)}, u32[]{:S(2)}) collective-permute-start(f32[768,128]{1,0:T(8,128)} %get-tuple-element.58), channel_id=1, source_target_pairs={{0,2},{4,6},{8,10},{12,14},{16,18},{20,22},{24,26},{28,30}} | collective-permute-start | bytes 1179656 | tf_op jit(solution)/shard_map/ppermute | solution.py:221
  16.0 2.1 %fusion.13 = (f32[768,128]{1,0:T(8,128)}, f32[768,128]{1,0:T(8,128)}) fusion(f32[1024,128]{1,0:T(8,128)} %param.10), kind=kLoop, calls=%fused_computation.46 | loop fusion | bytes 1572864 | tf_op jit(solution)/shard_map/slice | solution.py:220
  18.1 3.6 %collective-permute-start = (f32[768,128]{1,0:T(8,128)}, f32[768,128]{1,0:T(8,128)}, u32[]{:S(2)}, u32[]{:S(2)}) collective-permute-start(f32[768,128]{1,0:T(8,128)} %get-tuple-element.60), channel_id=1, source_target_pairs={{0,2},{4,6},{8,10},{12,14},{16,18},{20,22},{24,26},{28,30}} | collective-permute-start | bytes 1179656 | tf_op jit(solution)/shard_map/ppermute | solution.py:221
  23.7 1.4 fusion.7
  30.1 15.2 %collective-permute-done = f32[768,128]{1,0:T(8,128)} collective-permute-done((f32[768,128]{1,0:T(8,128)}, f32[768,128]{1,0:T(8,128)}, u32[]{:S(2)}, u32[]{:S(2)}) %collective-permute-start) | collective-permute-done | bytes 393248 | tf_op jit(solution)/shard_map/ppermute | solution.py:221
  48.3 1.7 dynamic-slice_select_fusion
  50.0 7.3 %shard_map.110 = (f32[2048,128]{1,0:T(8,128)}, f32[2048,128]{1,0:T(8,128)}, f32[2,512,128]{2,1,0:T(8,128)S(1)}, f32[8,128]{1,0:T(8,128)S(1)}) custom-call(s32[1]{0:T(128)} %bitcast.1.count_ref, f32[16,4]{1,0:T(8,128)S(1)} %copy.12.live_ref, bf16[4,2048,512]{2,1,0:T(8,128)(2,1)} %ratings_hbm.7, f32[2048,128]{1,0:T(8,128)} %get-tuple-element.66.fac_in, ...), custom_call_target="tpu_custom_call" | custom-call | tf_op jit(solution)/shard_map/pallas_call | solution.py:116
  57.3 18.0 %collective-permute-start.8 = (f32[2,512,128]{2,1,0:T(8,128)S(1)}, f32[2,512,128]{2,1,0:T(8,128)S(1)}, u32[]{:S(2)}, u32[]{:S(2)}) collective-permute-start(f32[2,512,128]{2,1,0:T(8,128)S(1)} %get-tuple-element.27), channel_id=1, source_target_pairs={{0,1},{1,2},{2,3},{3,4},{4,5},{5,6},{6,7},{7,8},{8,9},{9,10},{10,1... | collective-permute-start | bytes 1572872 | tf_op jit(solution)/shard_map/ppermute | solution.py:22
  75.4 8.2 %collective-permute-done.8.pair_in = f32[2,512,128]{2,1,0:T(8,128)S(1)} collective-permute-done((f32[2,512,128]{2,1,0:T(8,128)S(1)}, f32[2,512,128]{2,1,0:T(8,128)S(1)}, u32[]{:S(2)}, u32[]{:S(2)}) %collective-permute-start.8) | collective-permute-done | bytes 524320 | tf_op jit(solution)/shard_map/ppermute | solution.py:22
  83.6 7.3 %shard_map.111 = (f32[2048,128]{1,0:T(8,128)}, f32[2048,128]{1,0:T(8,128)}, f32[2,512,128]{2,1,0:T(8,128)S(1)}, f32[8,128]{1,0:T(8,128)S(1)}) custom-call(s32[1]{0:T(128)} %bitcast.1.count_ref, f32[16,4]{1,0:T(8,128)S(1)} %copy.13.live_ref, bf16[4,2048,512]{2,1,0:T(8,128)(2,1)} %ratings_hbm.7, f32[2048,128]{1,0:T(8,128)} %get-tuple-element.25.fac_in, ...), custom_call_target="tpu_custom_call" | custom-call | tf_op jit(solution)/shard_map/pallas_call | solution.py:116
  90.9 8.2 %collective-permute-start.9 = (f32[2,512,128]{2,1,0:T(8,128)S(1)}, f32[2,512,128]{2,1,0:T(8,128)S(1)}, u32[]{:S(2)}, u32[]{:S(2)}) collective-permute-start(f32[2,512,128]{2,1,0:T(8,128)S(1)} %get-tuple-element.31), channel_id=1, source_target_pairs={{0,1},{1,2},{2,3},{3,4},{4,5},{5,6},{6,7},{7,8},{8,9},{9,10},{10,1... | collective-permute-start | bytes 1572872 | tf_op jit(solution)/shard_map/ppermute | solution.py:22
  99.2 9.9 %collective-permute-done.9.pair_in = f32[2,512,128]{2,1,0:T(8,128)S(1)} collective-permute-done((f32[2,512,128]{2,1,0:T(8,128)S(1)}, f32[2,512,128]{2,1,0:T(8,128)S(1)}, u32[]{:S(2)}, u32[]{:S(2)}) %collective-permute-start.9) | collective-permute-done | bytes 524320 | tf_op jit(solution)/shard_map/ppermute | solution.py:22
  109.1 7.3 %shard_map.112 = (f32[2048,128]{1,0:T(8,128)}, f32[2048,128]{1,0:T(8,128)}, f32[2,512,128]{2,1,0:T(8,128)S(1)}, f32[8,128]{1,0:T(8,128)S(1)}) custom-call(s32[1]{0:T(128)} %bitcast.1.count_ref, f32[16,4]{1,0:T(8,128)S(1)} %copy.14.live_ref, bf16[4,2048,512]{2,1,0:T(8,128)(2,1)} %ratings_hbm.7, f32[2048,128]{1,0:T(8,128)} %get-tuple-element.29.fac_in, ...), custom_call_target="tpu_custom_call" | custom-call | tf_op jit(solution)/shard_map/pallas_call | solution.py:116
  116.4 5.5 %collective-permute-start.10 = (f32[2,512,128]{2,1,0:T(8,128)S(1)}, f32[2,512,128]{2,1,0:T(8,128)S(1)}, u32[]{:S(2)}, u32[]{:S(2)}) collective-permute-start(f32[2,512,128]{2,1,0:T(8,128)S(1)} %get-tuple-element.35), channel_id=1, source_target_pairs={{0,1},{1,2},{2,3},{3,4},{4,5},{5,6},{6,7},{7,8},{8,9},{9,10},{10,1... | collective-permute-start | bytes 1572872 | tf_op jit(solution)/shard_map/ppermute | solution.py:22
  123.8 11.9 %collective-permute-done.10.pair_in = f32[2,512,128]{2,1,0:T(8,128)S(1)} collective-permute-done((f32[2,512,128]{2,1,0:T(8,128)S(1)}, f32[2,512,128]{2,1,0:T(8,128)S(1)}, u32[]{:S(2)}, u32[]{:S(2)}) %collective-permute-start.10) | collective-permute-done | bytes 524320 | tf_op jit(solution)/shard_map/ppermute | solution.py:22
  135.7 7.3 %shard_map.113 = (f32[2048,128]{1,0:T(8,128)}, f32[2048,128]{1,0:T(8,128)}, f32[2,512,128]{2,1,0:T(8,128)S(1)}, f32[8,128]{1,0:T(8,128)S(1)}) custom-call(s32[1]{0:T(128)} %bitcast.1.count_ref, f32[16,4]{1,0:T(8,128)S(1)} %copy.15.live_ref, bf16[4,2048,512]{2,1,0:T(8,128)(2,1)} %ratings_hbm.7, f32[2048,128]{1,0:T(8,128)} %get-tuple-element.33.fac_in, ...), custom_call_target="tpu_custom_call" | custom-call | tf_op jit(solution)/shard_map/pallas_call | solution.py:116
  143.6 2.7 %concatenate.11 = f32[8]{0:T(128)S(1)} concatenate(f32[1]{0:T(128)} %bitcast.5, f32[1]{0:T(128)} %bitcast.7, f32[1]{0:T(128)} %bitcast.9, f32[1]{0:T(128)} %bitcast.11, f32[4]{0:T(128)S(1)} %broadcast_multiply_fusion), dimensions={0} | concatenate | bytes 64 | tf_op jit(solution)/shard_map/concatenate | solution.py:274
  146.8 12.9 %shard_map.114 = f32[8,128]{1,0:T(8,128)} custom-call(f32[8,128]{1,0:T(8,128)} %broadcast_in_dim.49.x_ref), custom_call_target="tpu_custom_call" | custom-call | tf_op jit(solution)/shard_map/pallas_call | solution.py:185
  161.8 1.4 collective-permute-start.16
  163.2 4.6 %collective-permute-start.17 = (f32[1024,128]{1,0:T(8,128)S(1)}, f32[1024,128]{1,0:T(8,128)S(1)}, u32[]{:S(2)}, u32[]{:S(2)}) collective-permute-start(f32[1024,128]{1,0:T(8,128)S(1)} %get-tuple-element.50), channel_id=1, source_target_pairs={{0,1},{1,2},{2,3},{4,5},{5,6},{6,7},{8,9},{9,10},{10,11},{12,13},{... | collective-permute-start | bytes 1572872 | tf_op jit(solution)/shard_map/ppermute | solution.py:236
  171.8 15.3 %collective-permute-done.15 = f32[768,128]{1,0:T(8,128)S(1)} collective-permute-done((f32[768,128]{1,0:T(8,128)S(1)}, f32[768,128]{1,0:T(8,128)S(1)}, u32[]{:S(2)}, u32[]{:S(2)}) %collective-permute-start.15) | collective-permute-done | bytes 393248 | tf_op jit(solution)/shard_map/ppermute | solution.py:236
  192.2 13.7 %collective-permute-done.11 = f32[768,128]{1,0:T(8,128)S(1)} collective-permute-done((f32[768,128]{1,0:T(8,128)S(1)}, f32[768,128]{1,0:T(8,128)S(1)}, u32[]{:S(2)}, u32[]{:S(2)}) %collective-permute-start.11) | collective-permute-done | bytes 393248 | tf_op jit(solution)/shard_map/ppermute | solution.py:236
  (79 shorter events, 27.1 us)
Async XLA Ops:
  0.6 47.2 %copy-start = (f32[1024,128]{1,0:T(8,128)S(1)}, f32[1024,128]{1,0:T(8,128)}, u32[]{:S(2)}) copy-start(f32[1024,128]{1,0:T(8,128)} %param.11) | copy-start | bytes 1572868
  0.6 28.2 %copy-start.1 = (f32[1024,128]{1,0:T(8,128)S(1)}, f32[1024,128]{1,0:T(8,128)}, u32[]{:S(2)}) copy-start(f32[1024,128]{1,0:T(8,128)} %param.10) | copy-start | bytes 1572868
  0.7 46.4 %collective-permute-start.5 = (f32[1024,128]{1,0:T(8,128)}, f32[1024,128]{1,0:T(8,128)S(1)}, u32[]{:S(2)}, u32[]{:S(2)}) collective-permute-start(f32[1024,128]{1,0:T(8,128)} %param.11), channel_id=1, source_target_pairs={{0,1},{1,2},{2,3},{4,5},{5,6},{6,7},{8,9},{9,10},{10,11},{12,13},{... | collective-permute-start | bytes 1572872 | tf_op jit(solution)/shard_map/ppermute | solution.py:221
  5.8 42.2 %collective-permute-start.6 = (f32[1024,128]{1,0:T(8,128)}, f32[1024,128]{1,0:T(8,128)S(1)}, u32[]{:S(2)}, u32[]{:S(2)}) collective-permute-start(f32[1024,128]{1,0:T(8,128)} %param.11), channel_id=1, source_target_pairs={{1,0},{2,1},{3,2},{5,4},{6,5},{7,6},{9,8},{10,9},{11,10},{13,12},{... | collective-permute-start | bytes 1572872 | tf_op jit(solution)/shard_map/ppermute | solution.py:221
  9.1 19.7 %collective-permute-start.4 = (f32[768,128]{1,0:T(8,128)}, f32[768,128]{1,0:T(8,128)S(1)}, u32[]{:S(2)}, u32[]{:S(2)}) collective-permute-start(f32[768,128]{1,0:T(8,128)} %get-tuple-element.58), channel_id=1, source_target_pairs={{0,2},{4,6},{8,10},{12,14},{16,18},{20,22},{24,26},{28,30}} | collective-permute-start | bytes 1179656 | tf_op jit(solution)/shard_map/ppermute | solution.py:221
  14.6 33.2 %collective-permute-start.1 = (f32[1024,128]{1,0:T(8,128)}, f32[1024,128]{1,0:T(8,128)S(1)}, u32[]{:S(2)}, u32[]{:S(2)}) collective-permute-start(f32[1024,128]{1,0:T(8,128)} %param.10), channel_id=1, source_target_pairs={{0,1},{1,2},{2,3},{4,5},{5,6},{6,7},{8,9},{9,10},{10,11},{12,13},{... | collective-permute-start | bytes 1572872 | tf_op jit(solution)/shard_map/ppermute | solution.py:221
  18.1 27.3 %collective-permute-start = (f32[768,128]{1,0:T(8,128)}, f32[768,128]{1,0:T(8,128)}, u32[]{:S(2)}, u32[]{:S(2)}) collective-permute-start(f32[768,128]{1,0:T(8,128)} %get-tuple-element.60), channel_id=1, source_target_pairs={{0,2},{4,6},{8,10},{12,14},{16,18},{20,22},{24,26},{28,30}} | collective-permute-start | bytes 1179656 | tf_op jit(solution)/shard_map/ppermute | solution.py:221
  28.8 19.3 %collective-permute-start.2 = (f32[1024,128]{1,0:T(8,128)S(1)}, f32[1024,128]{1,0:T(8,128)S(1)}, u32[]{:S(2)}, u32[]{:S(2)}) collective-permute-start(f32[1024,128]{1,0:T(8,128)S(1)} %copy-done.1), channel_id=1, source_target_pairs={{1,0},{2,1},{3,2},{5,4},{6,5},{7,6},{9,8},{10,9},{11,10},{13,12},{... | collective-permute-start | bytes 1572872 | tf_op jit(solution)/shard_map/ppermute | solution.py:221
  45.3 2.7 %collective-permute-start.7 = (f32[768,128]{1,0:T(8,128)}, f32[768,128]{1,0:T(8,128)S(1)}, u32[]{:S(2)}, u32[]{:S(2)}) collective-permute-start(f32[768,128]{1,0:T(8,128)} %get-tuple-element.57), channel_id=1, source_target_pairs={{3,1},{7,5},{11,9},{15,13},{19,17},{23,21},{27,25},{31,29}} | collective-permute-start | bytes 1179656 | tf_op jit(solution)/shard_map/ppermute | solution.py:221
  47.1 1.1 collective-permute-start.3
  50.0 25.3 %copy-start.5 = (f32[16,4]{0,1:T(4,128)S(1)}, f32[16,4]{0,1:T(4,128)}, u32[]{:S(2)}) copy-start(f32[16,4]{0,1:T(4,128)} %get-tuple-element.63) | copy-start | bytes 772
  57.3 26.2 %collective-permute-start.8 = (f32[2,512,128]{2,1,0:T(8,128)S(1)}, f32[2,512,128]{2,1,0:T(8,128)S(1)}, u32[]{:S(2)}, u32[]{:S(2)}) collective-permute-start(f32[2,512,128]{2,1,0:T(8,128)S(1)} %get-tuple-element.27), channel_id=1, source_target_pairs={{0,1},{1,2},{2,3},{3,4},{4,5},{5,6},{6,7},{7,8},{8,9},{9,10},{10,1... | collective-permute-start | bytes 1572872 | tf_op jit(solution)/shard_map/ppermute | solution.py:22
  83.6 15.5 %copy-start.4 = (f32[16,4]{0,1:T(4,128)S(1)}, f32[16,4]{0,1:T(4,128)}, u32[]{:S(2)}) copy-start(f32[16,4]{0,1:T(4,128)} %get-tuple-element.62) | copy-start | bytes 772
  90.9 18.2 %collective-permute-start.9 = (f32[2,512,128]{2,1,0:T(8,128)S(1)}, f32[2,512,128]{2,1,0:T(8,128)S(1)}, u32[]{:S(2)}, u32[]{:S(2)}) collective-permute-start(f32[2,512,128]{2,1,0:T(8,128)S(1)} %get-tuple-element.31), channel_id=1, source_target_pairs={{0,1},{1,2},{2,3},{3,4},{4,5},{5,6},{6,7},{7,8},{8,9},{9,10},{10,1... | collective-permute-start | bytes 1572872 | tf_op jit(solution)/shard_map/ppermute | solution.py:22
  116.4 19.3 %collective-permute-start.10 = (f32[2,512,128]{2,1,0:T(8,128)S(1)}, f32[2,512,128]{2,1,0:T(8,128)S(1)}, u32[]{:S(2)}, u32[]{:S(2)}) collective-permute-start(f32[2,512,128]{2,1,0:T(8,128)S(1)} %get-tuple-element.35), channel_id=1, source_target_pairs={{0,1},{1,2},{2,3},{3,4},{4,5},{5,6},{6,7},{7,8},{8,9},{9,10},{10,1... | collective-permute-start | bytes 1572872 | tf_op jit(solution)/shard_map/ppermute | solution.py:22
  143.0 18.3 %copy-start.3 = (f32[2048,128]{1,0:T(8,128)S(1)}, f32[2048,128]{1,0:T(8,128)}, u32[]{:S(2)}) copy-start(f32[2048,128]{1,0:T(8,128)} %get-tuple-element.40) | copy-start | bytes 3145732
  161.8 28.0 %collective-permute-start.16 = (f32[1024,128]{1,0:T(8,128)S(1)}, f32[1024,128]{1,0:T(8,128)S(1)}, u32[]{:S(2)}, u32[]{:S(2)}) collective-permute-start(f32[1024,128]{1,0:T(8,128)S(1)} %get-tuple-element.49), channel_id=1, source_target_pairs={{1,0},{2,1},{3,2},{5,4},{6,5},{7,6},{9,8},{10,9},{11,10},{13,12},{... | collective-permute-start | bytes 1572872 | tf_op jit(solution)/shard_map/ppermute | solution.py:236
  163.2 28.1 %collective-permute-start.17 = (f32[1024,128]{1,0:T(8,128)S(1)}, f32[1024,128]{1,0:T(8,128)S(1)}, u32[]{:S(2)}, u32[]{:S(2)}) collective-permute-start(f32[1024,128]{1,0:T(8,128)S(1)} %get-tuple-element.50), channel_id=1, source_target_pairs={{0,1},{1,2},{2,3},{4,5},{5,6},{6,7},{8,9},{9,10},{10,11},{12,13},{... | collective-permute-start | bytes 1572872 | tf_op jit(solution)/shard_map/ppermute | solution.py:236
  167.8 19.3 %collective-permute-start.15 = (f32[768,128]{1,0:T(8,128)S(1)}, f32[768,128]{1,0:T(8,128)S(1)}, u32[]{:S(2)}, u32[]{:S(2)}) collective-permute-start(f32[768,128]{1,0:T(8,128)S(1)} %get-tuple-element.47), channel_id=1, source_target_pairs={{2,0},{6,4},{10,8},{14,12},{18,16},{22,20},{26,24},{30,28}} | collective-permute-start | bytes 1179656 | tf_op jit(solution)/shard_map/ppermute | solution.py:236
  169.1 19.4 %collective-permute-start.18 = (f32[768,128]{1,0:T(8,128)S(1)}, f32[768,128]{1,0:T(8,128)S(1)}, u32[]{:S(2)}, u32[]{:S(2)}) collective-permute-start(f32[768,128]{1,0:T(8,128)S(1)} %get-tuple-element.48), channel_id=1, source_target_pairs={{1,3},{5,7},{9,11},{13,15},{17,19},{21,23},{25,27},{29,31}} | collective-permute-start | bytes 1179656 | tf_op jit(solution)/shard_map/ppermute | solution.py:236
  170.5 35.5 %collective-permute-start.12 = (f32[1024,128]{1,0:T(8,128)S(1)}, f32[1024,128]{1,0:T(8,128)S(1)}, u32[]{:S(2)}, u32[]{:S(2)}) collective-permute-start(f32[1024,128]{1,0:T(8,128)S(1)} %get-tuple-element.53), channel_id=1, source_target_pairs={{1,0},{2,1},{3,2},{5,4},{6,5},{7,6},{9,8},{10,9},{11,10},{13,12},{... | collective-permute-start | bytes 1572872 | tf_op jit(solution)/shard_map/ppermute | solution.py:236
  187.1 18.8 %collective-permute-start.13 = (f32[1024,128]{1,0:T(8,128)S(1)}, f32[1024,128]{1,0:T(8,128)S(1)}, u32[]{:S(2)}, u32[]{:S(2)}) collective-permute-start(f32[1024,128]{1,0:T(8,128)S(1)} %get-tuple-element.54), channel_id=1, source_target_pairs={{0,1},{1,2},{2,3},{4,5},{5,6},{6,7},{8,9},{9,10},{10,11},{12,13},{... | collective-permute-start | bytes 1572872 | tf_op jit(solution)/shard_map/ppermute | solution.py:236
  188.5 17.4 %collective-permute-start.11 = (f32[768,128]{1,0:T(8,128)S(1)}, f32[768,128]{1,0:T(8,128)S(1)}, u32[]{:S(2)}, u32[]{:S(2)}) collective-permute-start(f32[768,128]{1,0:T(8,128)S(1)} %get-tuple-element.51), channel_id=1, source_target_pairs={{2,0},{6,4},{10,8},{14,12},{18,16},{22,20},{26,24},{30,28}} | collective-permute-start | bytes 1179656 | tf_op jit(solution)/shard_map/ppermute | solution.py:236
  189.8 16.1 %collective-permute-start.14 = (f32[768,128]{1,0:T(8,128)S(1)}, f32[768,128]{1,0:T(8,128)S(1)}, u32[]{:S(2)}, u32[]{:S(2)}) collective-permute-start(f32[768,128]{1,0:T(8,128)S(1)} %get-tuple-element.52), channel_id=1, source_target_pairs={{1,3},{5,7},{9,11},{13,15},{17,19},{21,23},{25,27},{29,31}} | collective-permute-start | bytes 1179656 | tf_op jit(solution)/shard_map/ppermute | solution.py:236
  (2 other events, 21.4 us)

commit v5 on v4

--- a/solution.py
+++ b/solution.py
@@ -275,7 +275,7 @@
     sums = jnp.broadcast_to(jnp.pad(sums, (0, items.shape[1] - sums.shape[0]))[None, :], (8, items.shape[1]))
     totals = summed_everywhere(sums)[0]
     total_error, total_count = totals[:strata_count], totals[strata_count : 2 * strata_count]
-    losses, user_fac, user_acc = lax.optimization_barrier((total_error / total_count, user_fac, user_acc))
+    losses = total_error / total_count
     users_new = returned(jnp.where(row_valid, user_fac, 0.0), segments, tile_size, window)
     accum_new = returned(jnp.where(row_valid, user_acc, 0.0), segments, tile_size, window)
     return (users_new, accum_new, held_pair[0], held_pair[1], losses)

time: 210 us -> 208 us (level)
  starting transfers between devices: 63.8 us -> 47.5 us
  Pallas kernels: 42.1 us -> 49.2 us
  local copies, waits for them, and re-layouts: 12.1 us -> 17 us
  other arithmetic: 13 us -> 15.7 us
    ppermute x3, starting transfers between devices: 31.7 us -> 13.3 us  [passed_along(): return lax.ppermute(value, axis, pairs)]
    ppermute x8, waiting for transfers between devices: 29.1 us -> 20.8 us  [returned(): part = lax.ppermute(part, 'col', [(m, home) for home, m in pairs])]
    ppermute x3, waiting for transfers between devices: 29.9 us -> 37 us  [passed_along(): return lax.ppermute(value, axis, pairs)]
    pallas_call x1, Pallas kernels: 12.9 us -> 20 us  [summed_everywhere(): pl.pallas_call(functools.partial(sum_kernel, axes), out_shape=jax.ShapeDt...]
    slice x4, local copies, waits for them, and re-layouts: 0.25 us -> 4.2 us  [returned(): part = frame[at:at + length]]
    add x2, other arithmetic: 1.82 us -> 4.59 us  [returned(): total = part if total is None else total + part]
    ppermute x8, starting transfers between devices: 12.6 us -> 14.7 us  [returned(): part = lax.ppermute(part, 'col', [(m, home) for home, m in pairs])]
  transfers between devices with their start and end apart: 19 -> 19, of which waited for: 6 -> 6; matrix products, arithmetic and copies ran while one was open for 8% -> 12% of each run, Pallas kernels for 0% -> 10%
where the time goes in v5:
time: 208 us; the launch traced here: 204 us
  waiting for transfers between devices  73.1 us (35%)
  Pallas kernels  49.2 us (24%)
  starting transfers between devices  47.5 us (23%)
  local copies, waits for them, and re-layouts  17 us (8%)
  other arithmetic  15.7 us (8%)
    ppermute x3, waiting for transfers between devices, passed_along(): return lax.ppermute(value, axis, pairs)  37 us
    pallas_call x4, Pallas kernels, run_stratum(): pl.pallas_call(functools.partial(stratum_kernel, stratum, STEPS, chunks,...  29.2 us
    ppermute x8, waiting for transfers between devices, returned(): part = lax.ppermute(part, 'col', [(m, home) for home, m in pairs])  20.8 us
    pallas_call x1, Pallas kernels, summed_everywhere(): pl.pallas_call(functools.partial(sum_kernel, axes), out_shape=jax.ShapeDt...  20 us
    ppermute x8, starting transfers between devices, fetched(): parts.append(lax.ppermute(part, 'col', pairs) if step else part)  19.5 us
    ppermute x8, waiting for transfers between devices, fetched(): parts.append(lax.ppermute(part, 'col', pairs) if step else part)  15.2 us
    ppermute x8, starting transfers between devices, returned(): part = lax.ppermute(part, 'col', [(m, home) for home, m in pairs])  14.7 us
    ppermute x3, starting transfers between devices, passed_along(): return lax.ppermute(value, axis, pairs)  13.3 us
  transfers between devices with their start and end apart: 19, of which 6 were waited for; matrix products, arithmetic and copies ran while one was open for 12% of the time, Pallas kernels for 10%

profile of v5, /device:TPU:0, one launch (start us, length us, event | category | flops | bytes accessed | tf_op | source)
XLA Modules:
  0.0 204.1 jit_solution(5467860579706122809)
XLA Ops:
  0.7 5.1 %collective-permute-start.5 = (f32[1024,128]{1,0:T(8,128)}, f32[1024,128]{1,0:T(8,128)S(1)}, u32[]{:S(2)}, u32[]{:S(2)}) collective-permute-start(f32[1024,128]{1,0:T(8,128)} %param.11), channel_id=1, source_target_pairs={{0,1},{1,2},{2,3},{4,5},{5,6},{6,7},{8,9},{9,10},{10,11},{12,13},{... | collective-permute-start | bytes 1572872 | tf_op jit(solution)/shard_map/ppermute | solution.py:221
  7.1 2.1 %fusion.12 = (f32[768,128]{1,0:T(8,128)}, f32[768,128]{1,0:T(8,128)}) fusion(f32[1024,128]{1,0:T(8,128)} %param.11), kind=kLoop, calls=%fused_computation.45 | loop fusion | bytes 1572864 | tf_op jit(solution)/shard_map/slice | solution.py:220
  9.2 5.5 %collective-permute-start.4 = (f32[768,128]{1,0:T(8,128)}, f32[768,128]{1,0:T(8,128)S(1)}, u32[]{:S(2)}, u32[]{:S(2)}) collective-permute-start(f32[768,128]{1,0:T(8,128)} %get-tuple-element.52), channel_id=1, source_target_pairs={{0,2},{4,6},{8,10},{12,14},{16,18},{20,22},{24,26},{28,30}} | collective-permute-start | bytes 1179656 | tf_op jit(solution)/shard_map/ppermute | solution.py:221
  16.1 2.1 %fusion.13 = (f32[768,128]{1,0:T(8,128)}, f32[768,128]{1,0:T(8,128)}) fusion(f32[1024,128]{1,0:T(8,128)} %param.10), kind=kLoop, calls=%fused_computation.46 | loop fusion | bytes 1572864 | tf_op jit(solution)/shard_map/slice | solution.py:220
  18.1 3.6 %collective-permute-start = (f32[768,128]{1,0:T(8,128)}, f32[768,128]{1,0:T(8,128)}, u32[]{:S(2)}, u32[]{:S(2)}) collective-permute-start(f32[768,128]{1,0:T(8,128)} %get-tuple-element.54), channel_id=1, source_target_pairs={{0,2},{4,6},{8,10},{12,14},{16,18},{20,22},{24,26},{28,30}} | collective-permute-start | bytes 1179656 | tf_op jit(solution)/shard_map/ppermute | solution.py:221
  30.1 15.2 %collective-permute-done = f32[768,128]{1,0:T(8,128)} collective-permute-done((f32[768,128]{1,0:T(8,128)}, f32[768,128]{1,0:T(8,128)}, u32[]{:S(2)}, u32[]{:S(2)}) %collective-permute-start) | collective-permute-done | bytes 393248 | tf_op jit(solution)/shard_map/ppermute | solution.py:221
  48.3 1.6 dynamic-slice_select_fusion
  50.0 7.3 %shard_map.110 = (f32[2048,128]{1,0:T(8,128)}, f32[2048,128]{1,0:T(8,128)}, f32[2,512,128]{2,1,0:T(8,128)S(1)}, f32[8,128]{1,0:T(8,128)S(1)}) custom-call(s32[1]{0:T(128)} %bitcast.1.count_ref, f32[16,4]{1,0:T(8,128)S(1)} %copy.12.live_ref, bf16[4,2048,512]{2,1,0:T(8,128)(2,1)} %ratings_hbm.7, f32[2048,128]{1,0:T(8,128)} %get-tuple-element.60.fac_in, ...), custom_call_target="tpu_custom_call" | custom-call | tf_op jit(solution)/shard_map/pallas_call | solution.py:116
  57.3 12.3 %collective-permute-start.8 = (f32[2,512,128]{2,1,0:T(8,128)S(1)}, f32[2,512,128]{2,1,0:T(8,128)S(1)}, u32[]{:S(2)}, u32[]{:S(2)}) collective-permute-start(f32[2,512,128]{2,1,0:T(8,128)S(1)} %get-tuple-element.23), channel_id=1, source_target_pairs={{0,1},{1,2},{2,3},{3,4},{4,5},{5,6},{6,7},{7,8},{8,9},{9,10},{10,1... | collective-permute-start | bytes 1572872 | tf_op jit(solution)/shard_map/ppermute | solution.py:22
  69.7 11.7 %collective-permute-done.8.pair_in = f32[2,512,128]{2,1,0:T(8,128)S(1)} collective-permute-done((f32[2,512,128]{2,1,0:T(8,128)S(1)}, f32[2,512,128]{2,1,0:T(8,128)S(1)}, u32[]{:S(2)}, u32[]{:S(2)}) %collective-permute-start.8) | collective-permute-done | bytes 524320 | tf_op jit(solution)/shard_map/ppermute | solution.py:22
  81.4 7.3 %shard_map.111 = (f32[2048,128]{1,0:T(8,128)}, f32[2048,128]{1,0:T(8,128)}, f32[2,512,128]{2,1,0:T(8,128)S(1)}, f32[8,128]{1,0:T(8,128)S(1)}) custom-call(s32[1]{0:T(128)} %bitcast.1.count_ref, f32[16,4]{1,0:T(8,128)S(1)} %copy.13.live_ref, bf16[4,2048,512]{2,1,0:T(8,128)(2,1)} %ratings_hbm.7, f32[2048,128]{1,0:T(8,128)} %get-tuple-element.21.fac_in, ...), custom_call_target="tpu_custom_call" | custom-call | tf_op jit(solution)/shard_map/pallas_call | solution.py:116
  89.7 13.6 %collective-permute-done.9.pair_in = f32[2,512,128]{2,1,0:T(8,128)S(1)} collective-permute-done((f32[2,512,128]{2,1,0:T(8,128)S(1)}, f32[2,512,128]{2,1,0:T(8,128)S(1)}, u32[]{:S(2)}, u32[]{:S(2)}) %collective-permute-start.9) | collective-permute-done | bytes 524320 | tf_op jit(solution)/shard_map/ppermute | solution.py:22
  103.3 7.3 %shard_map.112 = (f32[2048,128]{1,0:T(8,128)}, f32[2048,128]{1,0:T(8,128)}, f32[2,512,128]{2,1,0:T(8,128)S(1)}, f32[8,128]{1,0:T(8,128)S(1)}) custom-call(s32[1]{0:T(128)} %bitcast.1.count_ref, f32[16,4]{1,0:T(8,128)S(1)} %copy.14.live_ref, bf16[4,2048,512]{2,1,0:T(8,128)(2,1)} %ratings_hbm.7, f32[2048,128]{1,0:T(8,128)} %get-tuple-element.24.fac_in, ...), custom_call_target="tpu_custom_call" | custom-call | tf_op jit(solution)/shard_map/pallas_call | solution.py:116
  112.6 11.8 %collective-permute-done.10.pair_in = f32[2,512,128]{2,1,0:T(8,128)S(1)} collective-permute-done((f32[2,512,128]{2,1,0:T(8,128)S(1)}, f32[2,512,128]{2,1,0:T(8,128)S(1)}, u32[]{:S(2)}, u32[]{:S(2)}) %collective-permute-start.10) | collective-permute-done | bytes 524320 | tf_op jit(solution)/shard_map/ppermute | solution.py:22
  124.4 7.3 %shard_map.113 = (f32[2048,128]{1,0:T(8,128)}, f32[2048,128]{1,0:T(8,128)}, f32[2,512,128]{2,1,0:T(8,128)S(1)}, f32[8,128]{1,0:T(8,128)S(1)}) custom-call(s32[1]{0:T(128)} %bitcast.1.count_ref, f32[16,4]{1,0:T(8,128)S(1)} %copy.15.live_ref, bf16[4,2048,512]{2,1,0:T(8,128)(2,1)} %ratings_hbm.7, f32[2048,128]{1,0:T(8,128)} %get-tuple-element.27.fac_in, ...), custom_call_target="tpu_custom_call" | custom-call | tf_op jit(solution)/shard_map/pallas_call | solution.py:116
  136.8 5.4 %collective-permute-start.17 = (f32[1024,128]{1,0:T(8,128)}, f32[1024,128]{1,0:T(8,128)}, u32[]{:S(2)}, u32[]{:S(2)}) collective-permute-start(f32[1024,128]{1,0:T(8,128)} %get-tuple-element.44), channel_id=1, source_target_pairs={{0,1},{1,2},{2,3},{4,5},{5,6},{6,7},{8,9},{9,10},{10,11},{12,13},{... | collective-permute-start | bytes 1572872 | tf_op jit(solution)/shard_map/ppermute | solution.py:236
  143.4 1.4 collective-permute-start.18
  148.7 12.5 %collective-permute-done.15 = f32[768,128]{1,0:T(8,128)S(1)} collective-permute-done((f32[768,128]{1,0:T(8,128)S(1)}, f32[768,128]{1,0:T(8,128)S(1)}, u32[]{:S(2)}, u32[]{:S(2)}) %collective-permute-start.15) | collective-permute-done | bytes 393248 | tf_op jit(solution)/shard_map/ppermute | solution.py:236
  161.2 2.1 %collective-permute-start.13 = (f32[1024,128]{1,0:T(8,128)}, f32[1024,128]{1,0:T(8,128)}, u32[]{:S(2)}, u32[]{:S(2)}) collective-permute-start(f32[1024,128]{1,0:T(8,128)} %get-tuple-element.48), channel_id=1, source_target_pairs={{0,1},{1,2},{2,3},{4,5},{5,6},{6,7},{8,9},{9,10},{10,11},{12,13},{... | collective-permute-start | bytes 1572872 | tf_op jit(solution)/shard_map/ppermute | solution.py:236
  164.7 2.5 %concatenate.11 = f32[8]{0:T(128)S(1)} concatenate(f32[1]{0:T(128)} %bitcast.10, f32[1]{0:T(128)} %bitcast.11, f32[1]{0:T(128)} %bitcast.12, f32[1]{0:T(128)} %bitcast.13, f32[4]{0:T(128)S(1)} %broadcast_multiply_fusion), dimensions={0} | concatenate | bytes 64 | tf_op jit(solution)/shard_map/concatenate | solution.py:274
  167.9 20.0 %shard_map.114 = f32[8,128]{1,0:T(8,128)} custom-call(f32[8,128]{1,0:T(8,128)} %broadcast_in_dim.49.x_ref), custom_call_target="tpu_custom_call" | custom-call | tf_op jit(solution)/shard_map/pallas_call | solution.py:185
  191.2 2.5 %fusion.1 = f32[1024,128]{1,0:T(8,128)} fusion(f32[1024,128]{1,0:T(8,128)} %collective-permute-done.17, f32[6656,128]{1,0:T(8,128)} %copy-done, f32[768,128]{1,0:T(8,128)} %collective-permute-done.18, f32[1024,128]{1,0:T(8,128)} %collective-permute-done.16, f32[768,128]{1,0:T(8,128)} %copy-done.5), kind=kLoop, calls=%fused_computation.6 | loop fusion | flops 524288 | bytes 2883584 | tf_op jit(solution)/shard_map/add | solution.py:238
  193.7 8.3 %collective-permute-done.11 = f32[768,128]{1,0:T(8,128)S(1)} collective-permute-done((f32[768,128]{1,0:T(8,128)}, f32[768,128]{1,0:T(8,128)S(1)}, u32[]{:S(2)}, u32[]{:S(2)}) %collective-permute-start.11) | collective-permute-done | bytes 393248 | tf_op jit(solution)/shard_map/ppermute | solution.py:236
  202.0 2.1 %fusion.3 = f32[1024,128]{1,0:T(8,128)} fusion(f32[1024,128]{1,0:T(8,128)} %collective-permute-done.13, f32[6656,128]{1,0:T(8,128)S(1)} %select_dynamic-update-slice_fusion.1, f32[768,128]{1,0:T(8,128)S(1)} %collective-permute-done.14, f32[1024,128]{1,0:T(8,128)} %collective-permute-done.12, f32[768,128]{1,0:T(8,128)S(1)} %collective-permute-done.11), kind=kLoop, calls=%fused_computation.9 | loop fusion | flops 524288 | bytes 2883584 | tf_op jit(solution)/shard_map/add | solution.py:238
  (83 shorter events, 31.8 us)
Async XLA Ops:
  0.6 47.2 %copy-start.1 = (f32[1024,128]{1,0:T(8,128)S(1)}, f32[1024,128]{1,0:T(8,128)}, u32[]{:S(2)}) copy-start(f32[1024,128]{1,0:T(8,128)} %param.11) | copy-start | bytes 1572868
  0.6 28.2 %copy-start.2 = (f32[1024,128]{1,0:T(8,128)S(1)}, f32[1024,128]{1,0:T(8,128)}, u32[]{:S(2)}) copy-start(f32[1024,128]{1,0:T(8,128)} %param.10) | copy-start | bytes 1572868
  0.7 46.4 %collective-permute-start.5 = (f32[1024,128]{1,0:T(8,128)}, f32[1024,128]{1,0:T(8,128)S(1)}, u32[]{:S(2)}, u32[]{:S(2)}) collective-permute-start(f32[1024,128]{1,0:T(8,128)} %param.11), channel_id=1, source_target_pairs={{0,1},{1,2},{2,3},{4,5},{5,6},{6,7},{8,9},{9,10},{10,11},{12,13},{... | collective-permute-start | bytes 1572872 | tf_op jit(solution)/shard_map/ppermute | solution.py:221
  5.8 42.2 %collective-permute-start.6 = (f32[1024,128]{1,0:T(8,128)}, f32[1024,128]{1,0:T(8,128)S(1)}, u32[]{:S(2)}, u32[]{:S(2)}) collective-permute-start(f32[1024,128]{1,0:T(8,128)} %param.11), channel_id=1, source_target_pairs={{1,0},{2,1},{3,2},{5,4},{6,5},{7,6},{9,8},{10,9},{11,10},{13,12},{... | collective-permute-start | bytes 1572872 | tf_op jit(solution)/shard_map/ppermute | solution.py:221
  9.2 19.6 %collective-permute-start.4 = (f32[768,128]{1,0:T(8,128)}, f32[768,128]{1,0:T(8,128)S(1)}, u32[]{:S(2)}, u32[]{:S(2)}) collective-permute-start(f32[768,128]{1,0:T(8,128)} %get-tuple-element.52), channel_id=1, source_target_pairs={{0,2},{4,6},{8,10},{12,14},{16,18},{20,22},{24,26},{28,30}} | collective-permute-start | bytes 1179656 | tf_op jit(solution)/shard_map/ppermute | solution.py:221
  14.7 33.1 %collective-permute-start.1 = (f32[1024,128]{1,0:T(8,128)}, f32[1024,128]{1,0:T(8,128)S(1)}, u32[]{:S(2)}, u32[]{:S(2)}) collective-permute-start(f32[1024,128]{1,0:T(8,128)} %param.10), channel_id=1, source_target_pairs={{0,1},{1,2},{2,3},{4,5},{5,6},{6,7},{8,9},{9,10},{10,11},{12,13},{... | collective-permute-start | bytes 1572872 | tf_op jit(solution)/shard_map/ppermute | solution.py:221
  18.1 27.2 %collective-permute-start = (f32[768,128]{1,0:T(8,128)}, f32[768,128]{1,0:T(8,128)}, u32[]{:S(2)}, u32[]{:S(2)}) collective-permute-start(f32[768,128]{1,0:T(8,128)} %get-tuple-element.54), channel_id=1, source_target_pairs={{0,2},{4,6},{8,10},{12,14},{16,18},{20,22},{24,26},{28,30}} | collective-permute-start | bytes 1179656 | tf_op jit(solution)/shard_map/ppermute | solution.py:221
  28.8 19.3 %collective-permute-start.2 = (f32[1024,128]{1,0:T(8,128)S(1)}, f32[1024,128]{1,0:T(8,128)S(1)}, u32[]{:S(2)}, u32[]{:S(2)}) collective-permute-start(f32[1024,128]{1,0:T(8,128)S(1)} %copy-done.2), channel_id=1, source_target_pairs={{1,0},{2,1},{3,2},{5,4},{6,5},{7,6},{9,8},{10,9},{11,10},{13,12},{... | collective-permute-start | bytes 1572872 | tf_op jit(solution)/shard_map/ppermute | solution.py:221
  45.3 2.7 %collective-permute-start.7 = (f32[768,128]{1,0:T(8,128)}, f32[768,128]{1,0:T(8,128)S(1)}, u32[]{:S(2)}, u32[]{:S(2)}) collective-permute-start(f32[768,128]{1,0:T(8,128)} %get-tuple-element.51), channel_id=1, source_target_pairs={{3,1},{7,5},{11,9},{15,13},{19,17},{23,21},{27,25},{31,29}} | collective-permute-start | bytes 1179656 | tf_op jit(solution)/shard_map/ppermute | solution.py:221
  47.1 1.1 collective-permute-start.3
  50.0 19.7 %copy-start.7 = (f32[16,4]{0,1:T(4,128)S(1)}, f32[16,4]{0,1:T(4,128)}, u32[]{:S(2)}) copy-start(f32[16,4]{0,1:T(4,128)} %get-tuple-element.56) | copy-start | bytes 772
  57.3 24.1 %collective-permute-start.8 = (f32[2,512,128]{2,1,0:T(8,128)S(1)}, f32[2,512,128]{2,1,0:T(8,128)S(1)}, u32[]{:S(2)}, u32[]{:S(2)}) collective-permute-start(f32[2,512,128]{2,1,0:T(8,128)S(1)} %get-tuple-element.23), channel_id=1, source_target_pairs={{0,1},{1,2},{2,3},{3,4},{4,5},{5,6},{6,7},{7,8},{8,9},{9,10},{10,1... | collective-permute-start | bytes 1572872 | tf_op jit(solution)/shard_map/ppermute | solution.py:22
  88.7 14.6 %collective-permute-start.9 = (f32[2,512,128]{2,1,0:T(8,128)S(1)}, f32[2,512,128]{2,1,0:T(8,128)S(1)}, u32[]{:S(2)}, u32[]{:S(2)}) collective-permute-start(f32[2,512,128]{2,1,0:T(8,128)S(1)} %get-tuple-element.26), channel_id=1, source_target_pairs={{0,1},{1,2},{2,3},{3,4},{4,5},{5,6},{6,7},{7,8},{8,9},{9,10},{10,1... | collective-permute-start | bytes 1572872 | tf_op jit(solution)/shard_map/ppermute | solution.py:22
  110.6 13.8 %collective-permute-start.10 = (f32[2,512,128]{2,1,0:T(8,128)S(1)}, f32[2,512,128]{2,1,0:T(8,128)S(1)}, u32[]{:S(2)}, u32[]{:S(2)}) collective-permute-start(f32[2,512,128]{2,1,0:T(8,128)S(1)} %get-tuple-element.29), channel_id=1, source_target_pairs={{0,1},{1,2},{2,3},{3,4},{4,5},{5,6},{6,7},{7,8},{8,9},{9,10},{10,1... | collective-permute-start | bytes 1572872 | tf_op jit(solution)/shard_map/ppermute | solution.py:22
  133.2 11.9 %copy-start = (f32[6656,128]{1,0:T(8,128)}, f32[6656,128]{1,0:T(8,128)S(1)}, u32[]{:S(2)}) copy-start(f32[6656,128]{1,0:T(8,128)S(1)} %select_dynamic-update-slice_fusion) | copy-start | bytes 10223620
  133.3 11.9 %copy-start.3 = (f32[2048,128]{1,0:T(8,128)S(1)}, f32[2048,128]{1,0:T(8,128)}, u32[]{:S(2)}) copy-start(f32[2048,128]{1,0:T(8,128)} %get-tuple-element.30) | copy-start | bytes 3145732
  135.5 53.7 %collective-permute-start.16 = (f32[1024,128]{1,0:T(8,128)}, f32[1024,128]{1,0:T(8,128)}, u32[]{:S(2)}, u32[]{:S(2)}) collective-permute-start(f32[1024,128]{1,0:T(8,128)} %get-tuple-element.43), channel_id=1, source_target_pairs={{1,0},{2,1},{3,2},{5,4},{6,5},{7,6},{9,8},{10,9},{11,10},{13,12},{... | collective-permute-start | bytes 1572872 | tf_op jit(solution)/shard_map/ppermute | solution.py:236
  136.8 54.4 %collective-permute-start.17 = (f32[1024,128]{1,0:T(8,128)}, f32[1024,128]{1,0:T(8,128)}, u32[]{:S(2)}, u32[]{:S(2)}) collective-permute-start(f32[1024,128]{1,0:T(8,128)} %get-tuple-element.44), channel_id=1, source_target_pairs={{0,1},{1,2},{2,3},{4,5},{5,6},{6,7},{8,9},{9,10},{10,11},{12,13},{... | collective-permute-start | bytes 1572872 | tf_op jit(solution)/shard_map/ppermute | solution.py:236
  142.1 19.1 %collective-permute-start.15 = (f32[768,128]{1,0:T(8,128)S(1)}, f32[768,128]{1,0:T(8,128)S(1)}, u32[]{:S(2)}, u32[]{:S(2)}) collective-permute-start(f32[768,128]{1,0:T(8,128)S(1)} %get-tuple-element.41), channel_id=1, source_target_pairs={{2,0},{6,4},{10,8},{14,12},{18,16},{22,20},{26,24},{30,28}} | collective-permute-start | bytes 1179656 | tf_op jit(solution)/shard_map/ppermute | solution.py:236
  143.4 44.4 %collective-permute-start.18 = (f32[768,128]{1,0:T(8,128)}, f32[768,128]{1,0:T(8,128)}, u32[]{:S(2)}, u32[]{:S(2)}) collective-permute-start(f32[768,128]{1,0:T(8,128)} %get-tuple-element.42), channel_id=1, source_target_pairs={{1,3},{5,7},{9,11},{13,15},{17,19},{21,23},{25,27},{29,31}} | collective-permute-start | bytes 1179656 | tf_op jit(solution)/shard_map/ppermute | solution.py:236
  147.4 54.6 %collective-permute-start.12 = (f32[1024,128]{1,0:T(8,128)}, f32[1024,128]{1,0:T(8,128)}, u32[]{:S(2)}, u32[]{:S(2)}) collective-permute-start(f32[1024,128]{1,0:T(8,128)} %get-tuple-element.47), channel_id=1, source_target_pairs={{1,0},{2,1},{3,2},{5,4},{6,5},{7,6},{9,8},{10,9},{11,10},{13,12},{... | collective-permute-start | bytes 1572872 | tf_op jit(solution)/shard_map/ppermute | solution.py:236
  161.2 40.8 %collective-permute-start.13 = (f32[1024,128]{1,0:T(8,128)}, f32[1024,128]{1,0:T(8,128)}, u32[]{:S(2)}, u32[]{:S(2)}) collective-permute-start(f32[1024,128]{1,0:T(8,128)} %get-tuple-element.48), channel_id=1, source_target_pairs={{0,1},{1,2},{2,3},{4,5},{5,6},{6,7},{8,9},{9,10},{10,11},{12,13},{... | collective-permute-start | bytes 1572872 | tf_op jit(solution)/shard_map/ppermute | solution.py:236
  187.9 14.1 %collective-permute-start.11 = (f32[768,128]{1,0:T(8,128)}, f32[768,128]{1,0:T(8,128)S(1)}, u32[]{:S(2)}, u32[]{:S(2)}) collective-permute-start(f32[768,128]{1,0:T(8,128)} %get-tuple-element.45), channel_id=1, source_target_pairs={{2,0},{6,4},{10,8},{14,12},{18,16},{22,20},{26,24},{30,28}} | collective-permute-start | bytes 1179656 | tf_op jit(solution)/shard_map/ppermute | solution.py:236
  189.2 12.8 %collective-permute-start.14 = (f32[768,128]{1,0:T(8,128)}, f32[768,128]{1,0:T(8,128)S(1)}, u32[]{:S(2)}, u32[]{:S(2)}) collective-permute-start(f32[768,128]{1,0:T(8,128)} %get-tuple-element.46), channel_id=1, source_target_pairs={{1,3},{5,7},{9,11},{13,15},{17,19},{21,23},{25,27},{29,31}} | collective-permute-start | bytes 1179656 | tf_op jit(solution)/shard_map/ppermute | solution.py:236
  (4 other events, 19.8 us)
